TPU v7x, 256 devices: a whole 4x4x8 slice. The times are simulated.
256 devices in a mesh: seq: 32 (over x, z), head: 8 (over y, core).
Axes of the slice: x: 4, y: 4, z: 8, core: 2. Of those that a mesh axis runs over, the one named last changes fastest.
Arguments:
- x_values: bfloat16 [32768, 8192], P('seq', 'head'), may hold values from -6 to 6
- b_values: bfloat16 [32768, 1024], P('seq', 'head'), may hold values from -6 to 6
- c_values: bfloat16 [32768, 1024], P('seq', 'head'), may hold values from -6 to 6
- z_values: bfloat16 [32768, 8192], P('seq', 'head'), may hold values from -6 to 6
- time_steps: float32 [32768, 128], P('seq', 'head'), may hold values from 0 to 0.35, as said below
- decay_rate: float32 [128], P('head'), may hold values from 0.5 to 2
- skip_gain: float32 [128], P('head'), may hold values from 0.5 to 1.5
- conv_x: bfloat16 [4, 8192], P(None, 'head'), may hold values from -3 to 3
- conv_bc: bfloat16 [2, 4, 1024], P(None, None, 'head'), may hold values from -3 to 3
- norm_gain: float32 [8192], P('head'), may hold values from 0.5 to 13, as said below
- rollout: bfloat16 [32768, 8192], P('seq', 'head'), may hold values from -6 to 6
- seq_spans: int32 [4], replicated, may hold values from 1 to 64, 128 in all
Outputs:
- normed: bfloat16 [32768, 8192], P('seq', 'head')
- rel_error: float32 [32768], P('seq')
Inputs may be any that keep to these rules, and one draw needn't show every extreme that they name: `time_steps`: positive step sizes. `norm_gain`: positive gains. `seq_spans`: the spans of all sequences sum to 128.
All inputs are finite; a program needn't handle non-finite values.
Results may differ from a plain program's by a relative error of at most 0.0046.
Values may be sent and summed in bfloat16 or wider, within the bound.
No kernel may reach another device: no remote copies, remote signals or barrier semaphores. Data moves between devices by JAX's collectives and lax.ppermute only.
A program may use at most 128 MiB of HBM per device.

v0:
```python
import jax
import jax.numpy as jnp
from jax import lax
from jax.sharding import PartitionSpec as P

HEADS = 128
HEAD_DIM = 64
STATE = 128
GROUPS = 8
CONV_K = 4
SPAN = 256


def shifted_2(block, axis, distance):
    devices = range(lax.axis_size(axis))
    route = [(i - distance, i) for i in devices if i - distance in devices]
    return lax.ppermute(block, axis, route)


def causal_conv(
    payload_vector_items, boundary_rows, weight, slot_offset_within_sequence, begin_token
):
    reach = CONV_K - 1
    extended = jnp.concatenate([boundary_rows, payload_vector_items], axis=0)
    count = payload_vector_items.shape[0]
    summed = jnp.zeros(payload_vector_items.shape, jnp.float32)
    for offset in range(CONV_K):
        shifted = extended[reach - offset : reach - offset + count]
        inside = (slot_offset_within_sequence - offset >= begin_token)[:, None]
        summed = summed + jnp.where(inside, shifted.astype(jnp.float32), 0.0) * weight[
            CONV_K - 1 - offset
        ].astype(jnp.float32)
    return jax.nn.silu(summed).astype(jnp.bfloat16)


def compose_flat(earlier, later):
    return (earlier[0] * later[0], later[0] * earlier[1] + later[1])


def shards(
    x_values,
    b_values,
    c_values,
    z_values,
    time_steps,
    decay_rate,
    skip_gain,
    conv_x,
    conv_bc,
    norm_gain,
    rollout,
    seq_spans,
):
    shard_count = lax.axis_size("seq")
    row_count = x_values.shape[0]
    slot_count = row_count // SPAN
    heads_here = decay_rate.shape[0]
    group_heads = HEADS // GROUPS
    groups_here = heads_here // group_heads
    spans_all = slot_count * shard_count
    first_span = lax.axis_index("seq") * slot_count
    starts = jnp.cumsum(seq_spans, dtype=jnp.int32) - seq_spans
    local_ids = first_span + jnp.arange(slot_count, dtype=jnp.int32)
    begin_here = jnp.max(
        jnp.where(local_ids[:, None] >= starts[None, :], starts[None, :], 0), axis=1
    )
    begin_token = jnp.repeat(begin_here * SPAN, SPAN)
    slot_offset_within_sequence = first_span * SPAN + jnp.arange(row_count, dtype=jnp.int32)
    reach = CONV_K - 1
    x_edge, b_edge, c_edge = shifted_2(
        (
            x_values[row_count - reach :],
            b_values[row_count - reach :],
            c_values[row_count - reach :],
        ),
        "seq",
        1,
    )
    x_conv = causal_conv(x_values, x_edge, conv_x, slot_offset_within_sequence, begin_token)
    b_conv = causal_conv(b_values, b_edge, conv_bc[0], slot_offset_within_sequence, begin_token)
    readout_filter_output = causal_conv(
        c_values, c_edge, conv_bc[1], slot_offset_within_sequence, begin_token
    )
    x_trans = jnp.transpose(
        x_conv.reshape(slot_count, SPAN, groups_here, group_heads, HEAD_DIM), (0, 2, 3, 4, 1)
    )
    b_trans = jnp.transpose(b_conv.reshape(slot_count, SPAN, groups_here, STATE), (0, 2, 3, 1))
    c_trans = jnp.transpose(
        readout_filter_output.reshape(slot_count, SPAN, groups_here, STATE), (0, 2, 3, 1)
    )
    steps_here = time_steps.reshape(slot_count, SPAN, heads_here)
    cumulated = jnp.cumsum(-steps_here * decay_rate[None, None, :], axis=1)
    by_head = jnp.transpose(cumulated, (0, 2, 1)).reshape(
        slot_count, groups_here, group_heads, SPAN
    )
    step_head = jnp.transpose(steps_here, (0, 2, 1)).reshape(
        slot_count, groups_here, group_heads, SPAN
    )
    past_only_filter = jnp.arange(SPAN)[:, None] >= jnp.arange(SPAN)[None, :]
    attention_weights_matrix = jnp.einsum(
        "sgnt,sgnu->sgtu", c_trans, b_trans, preferred_element_type=jnp.float32
    )
    spread_log = by_head[..., :, None] - by_head[..., None, :]
    mixing = jnp.where(
        past_only_filter,
        attention_weights_matrix[:, :, None]
        * jnp.exp(jnp.where(past_only_filter, spread_log, 0.0))
        * step_head[..., None, :],
        0.0,
    ).astype(jnp.bfloat16)
    mixed = jnp.einsum("sgqpu,sgqtu->sgqpt", x_trans, mixing, preferred_element_type=jnp.float32)
    weights = jnp.exp(by_head[..., -1:] - by_head) * step_head
    decayed = (b_trans[:, :, None, :, :] * weights[:, :, :, None, :]).astype(jnp.bfloat16)
    span_state = jnp.einsum(
        "sgqpu,sgqnu->sgqpn", x_trans, decayed, preferred_element_type=jnp.float32
    ).reshape(slot_count, heads_here, HEAD_DIM, STATE)
    span_decay = jnp.exp(cumulated[:, -1, :])
    flat_state = span_state.reshape(slot_count, heads_here * HEAD_DIM * STATE)
    spread = lax.all_to_all(flat_state, "seq", split_axis=1, concat_axis=0, tiled=True)
    piece_width = spread.shape[1]
    decay_all = lax.all_gather(span_decay, "seq", axis=0, tiled=True)
    entry_index = lax.axis_index("seq") * piece_width + jnp.arange(piece_width, dtype=jnp.int32)
    one_hot = (
        entry_index[None, :] // (STATE * HEAD_DIM)
        == jnp.arange(heads_here, dtype=jnp.int32)[:, None]
    ).astype(jnp.float32)
    span_ids = jnp.arange(spans_all, dtype=jnp.int32)
    keep_all = jnp.where(jnp.any(span_ids[:, None] == starts[None, :], axis=1), 0.0, 1.0).astype(
        jnp.float32
    )[:, None]
    factor = jnp.dot(decay_all, one_hot, precision=lax.Precision.HIGHEST) * keep_all
    ending = lax.associative_scan(compose_flat, (factor, spread), axis=0)[1]
    before_span = (
        jnp.concatenate([jnp.zeros((1, piece_width), jnp.float32), ending[: spans_all - 1]], axis=0)
        * keep_all
    )
    incoming_sequence_flag = lax.all_to_all(
        before_span.astype(jnp.bfloat16), "seq", split_axis=0, concat_axis=1, tiled=True
    ).astype(before_span.dtype)
    state_read = incoming_sequence_flag.astype(jnp.bfloat16).reshape(
        slot_count, groups_here, group_heads, HEAD_DIM, STATE
    )
    carried = jnp.einsum(
        "sgqpn,sgnt->sgqpt", state_read, c_trans, preferred_element_type=jnp.float32
    )
    mixed = mixed + jnp.exp(by_head)[:, :, :, None, :] * carried
    mixed = mixed + skip_gain.reshape(groups_here, group_heads)[:, :, None, None] * x_trans.astype(
        jnp.float32
    )
    z_trans = jnp.transpose(
        z_values.reshape(slot_count, SPAN, groups_here, group_heads, HEAD_DIM), (0, 2, 3, 4, 1)
    )
    gated = mixed * jax.nn.silu(z_trans.astype(jnp.float32))
    square_mean = jnp.mean(gated * gated, axis=(2, 3), keepdims=True)
    gain_trans = norm_gain.reshape(groups_here, group_heads, HEAD_DIM)[:, :, :, None]
    normed_trans = (gated * lax.rsqrt(square_mean + 1e-05) * gain_trans).astype(jnp.bfloat16)
    normed = jnp.transpose(normed_trans, (0, 4, 1, 2, 3)).reshape(row_count, heads_here * HEAD_DIM)
    roll_float = rollout.astype(jnp.float32)
    deviation = normed.astype(jnp.float32) - roll_float
    dev_sums, roll_sums = lax.psum(
        (jnp.sum(deviation * deviation, axis=1), jnp.sum(roll_float * roll_float, axis=1)), "head"
    )
    return (normed, jnp.sqrt(dev_sums / (roll_sums + 1e-06)))


def solution(mesh):
    placed = (
        P("seq", "head"),
        P("seq", "head"),
        P("seq", "head"),
        P("seq", "head"),
        P("seq", "head"),
        P("head"),
        P("head"),
        P(None, "head"),
        P(None, None, "head"),
        P("head"),
        P("seq", "head"),
        P(),
    )
    return jax.shard_map(
        shards, mesh=mesh, in_specs=placed, out_specs=(P("seq", "head"), P("seq")), check_vma=False
    )
```

profile of v0, /device:TPU:1, one launch (start us, length us, event | category | flops | bytes accessed | tf_op | source)
XLA Modules:
  0.0 330.4 jit_solution(13748498239813371299)
XLA Ops:
  1.3 4.4 %collective-permute-start.2 = (bf16[3,128]{1,0:T(4,128)(2,1)S(1)}, bf16[3,128]{1,0:T(4,128)(2,1)S(1)}, u32[]{:S(2)}, u32[]{:S(2)}) collective-permute-start(bf16[3,128]{1,0:T(4,128)(2,1)S(1)} %slice.281), channel_id=1, source_target_pairs={{0,8},{8,16},{16,24},{24,32},{32,40},{40,48},{48,56},{56,64},{64,7... | collective-permute-start | bytes 2312 | tf_op jit(solution)/shard_map/ppermute | solution.py:17
  6.4 3.5 %collective-permute-start = (bf16[3,1024]{1,0:T(4,128)(2,1)S(1)}, bf16[3,1024]{1,0:T(4,128)(2,1)S(1)}, u32[]{:S(2)}, u32[]{:S(2)}) collective-permute-start(bf16[3,1024]{1,0:T(4,128)(2,1)S(1)} %slice.265), channel_id=1, source_target_pairs={{0,8},{8,16},{16,24},{24,32},{32,40},{40,48},{48,56},{56,64},{64,7... | collective-permute-start | bytes 18440 | tf_op jit(solution)/shard_map/ppermute | solution.py:17
  23.4 9.0 %multiply_convert_fusion.3 = bf16[1024,1024]{1,0:T(8,128)(2,1)S(1)} fusion(bf16[1024,1024]{1,0:T(8,128)(2,1)} %param.12, bf16[3,1024]{1,0:T(4,128)(2,1)S(1)} %collective-permute-done, f32[1024]{0:T(1024)S(1)} %bitcast.142, f32[1024]{0:T(1024)S(1)} %bitcast.143, f32[1024]{0:T(1024)S(1)} %bitcast.141, f32[1024]{0:T(1024)S(1)} %bitcast.140, ...), kind=kLoop, calls=%fused_computation.27 | loop fusion | flops 30408704 | bytes 4220928 | tf_op jit(solution)/shard_map/convert_element_type | solution.py:33
  32.3 4.0 %reshape.394 = bf16[4,256,1,16,64]{4,3,1,0,2:T(8,128)(2,1)} reshape(bf16[1024,1024]{1,0:T(8,128)(2,1)S(1)} %multiply_convert_fusion.3) | data formatting | bytes 4194304 | tf_op jit(solution)/shard_map/reshape | solution.py:85
  36.3 4.9 %copy.110 = bf16[4,256,1,16,64]{1,4,3,0,2:T(8,128)(2,1)S(1)} copy(bf16[4,256,1,16,64]{4,3,1,0,2:T(8,128)(2,1)} %reshape.394) | data formatting | bytes 4194304 | tf_op jit(solution)/shard_map/reshape | solution.py:85
  49.9 9.4 %all-to-all-start = ((f32[4,32,4096]{2,0,1:T(4,128)}), f32[4,32,4096]{2,0,1:T(4,128)}, u32[]{:S(2)}, u32[]{:S(2)}) async-start(f32[4,32,4096]{2,0,1:T(4,128)} %copy.121), calls=%async_computation | async-start | bytes 4194304 | tf_op jit(solution)/shard_map/all_to_all | solution.py:119
  59.6 77.7 %all-gather = f32[128,1,16]{2,1,0:T(1,128)S(1)} all-gather(f32[4,1,16]{2,1,0:T(1,128)S(1)} %bitcast.145), channel_id=2, replica_groups=mesh['seq'=32,'head'=8] {'seq'}, dimensions={0}, use_global_device_ids=true | all-gather | bytes 8448 | tf_op jit(solution)/shard_map/all_gather | solution.py:121
  144.2 3.0 slice.293
  149.2 2.9 slice.295
  155.0 3.4 %fusion.47 = (f32[64,4096]{1,0:T(8,128)}, f32[64,4096]{1,0:T(8,128)S(1)}) fusion(f32[64,4096]{1,0:T(8,128)} %slice.298, f32[64,4096]{1,0:T(8,128)} %slice.294, f32[64,4096]{1,0:T(8,128)} %slice.296, f32[64,4096]{1,0:T(8,128)} %slice.295), kind=kLoop, calls=%fused_computation.134 | loop fusion | flops 786432 | bytes 6291456 | tf_op jit(solution)/shard_map/mul | solution.py:37
  161.4 3.3 slice.300
  164.6 3.3 slice.304
  214.9 3.3 %slice.299 = f32[31,4096]{1,0:T(8,128)} slice(f32[64,4096]{1,0:T(8,128)} %get-tuple-element.16), slice={[2:64:2], [0:4096:1]} | slice | bytes 1015808 | tf_op jit(solution)/shard_map/slice | solution.py:132
  219.8 3.0 slice.342
  232.9 8.6 %pad.156 = f32[128,4096]{1,0:T(8,128)} pad(f32[64,4096]{1,0:T(8,128)} %add.257, f32[]{:T(128)} %constant.56.clone.1), padding=1_0_1x0_0_0 | pad | bytes 3145732
  243.1 4.9 %pad.83 = f32[127,4096]{1,0:T(8,128)} pad(f32[64,4096]{1,0:T(8,128)S(1)} %pad_maximum_fusion.1, f32[]{:T(128)} %constant.56.clone.1), padding=0_0_1x0_0_0 | pad | bytes 3129348 | tf_op jit(solution)/shard_map/slice | solution.py:134
  251.3 6.6 %all-to-all-start.1 = ((bf16[32,4,4096]{2,1,0:T(4,128)(2,1)}), bf16[32,4,4096]{2,1,0:T(4,128)(2,1)S(1)}, u32[]{:S(2)}, u32[]{:S(2)}) async-start(bf16[32,4,4096]{2,1,0:T(4,128)(2,1)} %all_to_all.30), calls=%async_computation.1 | async-start | bytes 2097152 | tf_op jit(solution)/shard_map/all_to_all | solution.py:137
  259.2 3.7 %collective-permute-start.1 = (bf16[3,128]{1,0:T(4,128)(2,1)}, bf16[3,128]{1,0:T(4,128)(2,1)}, u32[]{:S(2)}, u32[]{:S(2)}) collective-permute-start(bf16[3,128]{1,0:T(4,128)(2,1)} %slice.273), channel_id=1, source_target_pairs={{0,8},{8,16},{16,24},{24,32},{32,40},{40,48},{48,56},{56,64},{64,7... | collective-permute-start | bytes 2312 | tf_op jit(solution)/shard_map/ppermute | solution.py:17
  263.5 4.4 %reshape.396 = f32[4,256,1,16,64]{4,3,1,0,2:T(8,128)} reshape(bf16[1024,1024]{1,0:T(8,128)(2,1)S(1)} %copy-done.3) | data formatting | bytes 6291456 | tf_op jit(solution)/shard_map/convert_element_type | solution.py:153
  268.0 7.9 %copy.127 = f32[4,256,1,16,64]{1,4,3,0,2:T(8,128)} copy(f32[4,256,1,16,64]{4,3,1,0,2:T(8,128)} %reshape.396) | data formatting | bytes 8388608 | tf_op jit(solution)/shard_map/convert_element_type | solution.py:153
  279.2 3.3 %multiply_convert_fusion.6 = bf16[1024,128]{1,0:T(8,128)(2,1)S(1)} fusion(bf16[1024,128]{1,0:T(8,128)(2,1)} %param.14, bf16[3,128]{1,0:T(4,128)(2,1)} %collective-permute-done.1, f32[128]{0:T(128)} %get-tuple-element.42, f32[128]{0:T(128)} %get-tuple-element.43, f32[128]{0:T(128)} %get-tuple-element.44, f32[128]{0:T(128)} %get-tuple-element.45, ...), kind=kLoop, calls=%fused_computation.46 | loop fusion | flops 3801088 | bytes 531200 | tf_op jit(solution)/shard_map/convert_element_type | solution.py:33
  283.0 7.3 %fusion = f32[4,16,64,256]{3,2,1,0:T(8,128)} fusion(f32[4,16,256]{2,1,0:T(8,128)} %bitcast.139, f32[4,16,256]{2,1,0:T(8,128)S(1)} %copy-done.12, f32[4,256,256]{2,1,0:T(8,128)S(1)} %fusion.30, pred[256,256]{1,0:T(8,128)(4,1)S(1)} %iota_compare_fusion.1, bf16[4,256,1,16,64]{1,4,3,0,2:T(8,128)(2,1)} %copy-done.4), kind=kOutput, calls=%fused_computation.1 | convolution fusion | flops 562036736 | bytes 7536640 | tf_op jit(solution)/shard_map/sgqpu,sgqtu->sgqpt/dot_general | solution.py:111
  291.5 5.1 %multiply_reduce_fusion = (f32[4,256]{1,0:T(4,128)S(1)}, f32[4,1,16,64,256]{4,3,2,0,1:T(8,128)S(1)}) fusion(f32[4,256,1,16,64]{1,4,3,0,2:T(8,128)} %copy.127, bf16[4,256,1,16,64]{1,4,3,0,2:T(8,128)(2,1)} %copy-done.4, f32[16]{0:T(128)S(1)} %copy-done.23, f32[4,16,64,256]{3,2,1,0:T(8,128)} %fusion, bf16[4,16,64,128]{3,2,1,0:T(8,128)(2,1)S(1)} %reshape.377, ...), kind=kOutput, calls=%fused_computation.24 | convolution fusion | flops 281017344 | bytes 16060480 | tf_op jit(solution)/shard_map/sgqpn,sgnt->sgqpt/dot_general | solution.py:143
  304.6 25.2 %all-reduce.15 = (f32[1024]{0:T(1024)S(1)}, f32[1024]{0:T(1024)S(1)}) all-reduce(f32[1024]{0:T(1024)S(1)} %get-tuple-element.13, f32[1024]{0:T(1024)S(1)} %get-tuple-element.12), channel_id=1, replica_groups=mesh['seq'=32,'head'=8] {'head'}, use_global_device_ids=true, to_apply=%region_7.8 | all-reduce | flops 2048 | bytes 16384 | tf_op jit(solution)/shard_map/psum | solution.py:160
  (180 shorter events, 117.0 us)
Async XLA Ops:
  1.3 18.9 %collective-permute-start.2 = (bf16[3,128]{1,0:T(4,128)(2,1)S(1)}, bf16[3,128]{1,0:T(4,128)(2,1)S(1)}, u32[]{:S(2)}, u32[]{:S(2)}) collective-permute-start(bf16[3,128]{1,0:T(4,128)(2,1)S(1)} %slice.281), channel_id=1, source_target_pairs={{0,8},{8,16},{16,24},{24,32},{32,40},{40,48},{48,56},{56,64},{64,7... | collective-permute-start | bytes 2312 | tf_op jit(solution)/shard_map/ppermute | solution.py:17
  6.4 16.9 %collective-permute-start = (bf16[3,1024]{1,0:T(4,128)(2,1)S(1)}, bf16[3,1024]{1,0:T(4,128)(2,1)S(1)}, u32[]{:S(2)}, u32[]{:S(2)}) collective-permute-start(bf16[3,1024]{1,0:T(4,128)(2,1)S(1)} %slice.265), channel_id=1, source_target_pairs={{0,8},{8,16},{16,24},{24,32},{32,40},{40,48},{48,56},{56,64},{64,7... | collective-permute-start | bytes 18440 | tf_op jit(solution)/shard_map/ppermute | solution.py:17
  17.2 19.2 %copy-start.15 = (pred[1024]{0:T(1024)(128)(4,1)}, pred[1024]{0:T(1024)(128)(4,1)S(1)}, u32[]{:S(2)}) copy-start(pred[1024]{0:T(1024)(128)(4,1)S(1)} %get-tuple-element.36) | copy-start | bytes 3076
  17.2 19.1 %copy-start.17 = (pred[1024]{0:T(1024)(128)(4,1)}, pred[1024]{0:T(1024)(128)(4,1)S(1)}, u32[]{:S(2)}) copy-start(pred[1024]{0:T(1024)(128)(4,1)S(1)} %get-tuple-element.37) | copy-start | bytes 3076
  17.2 19.1 %copy-start.19 = (pred[1024]{0:T(1024)(128)(4,1)}, pred[1024]{0:T(1024)(128)(4,1)S(1)}, u32[]{:S(2)}) copy-start(pred[1024]{0:T(1024)(128)(4,1)S(1)} %get-tuple-element.38) | copy-start | bytes 3076
  17.2 19.1 %copy-start.20 = (pred[1024]{0:T(1024)(128)(4,1)}, pred[1024]{0:T(1024)(128)(4,1)S(1)}, u32[]{:S(2)}) copy-start(pred[1024]{0:T(1024)(128)(4,1)S(1)} %get-tuple-element.39) | copy-start | bytes 3076
  49.9 97.3 %all-to-all-start = ((f32[4,32,4096]{2,0,1:T(4,128)}), f32[4,32,4096]{2,0,1:T(4,128)}, u32[]{:S(2)}, u32[]{:S(2)}) async-start(f32[4,32,4096]{2,0,1:T(4,128)} %copy.121), calls=%async_computation | async-start | bytes 4194304 | tf_op jit(solution)/shard_map/all_to_all | solution.py:119
  59.3 87.8 %copy-start.11 = (f32[4,16,256]{2,1,0:T(8,128)}, f32[4,16,256]{2,1,0:T(8,128)S(1)}, u32[]{:S(2)}) copy-start(f32[4,16,256]{2,1,0:T(8,128)S(1)} %copy_bitcast_fusion) | copy-start | bytes 196612
  137.5 9.7 %copy-start.21 = (f32[128]{0:T(128)}, f32[128]{0:T(128)S(1)}, u32[]{:S(2)}) copy-start(f32[128]{0:T(128)S(1)} %broadcast_select_fusion) | copy-start | bytes 1540
  149.2 73.6 %copy-start = (f32[128,4096]{1,0:T(8,128)}, f32[128,4096]{1,0:T(8,128)S(1)}, u32[]{:S(2)}) copy-start(f32[128,4096]{1,0:T(8,128)S(1)} %all_to_all.29) | copy-start | bytes 6291460
  219.7 7.6 %copy-start.13 = (f32[1,4096]{1,0:T(1,128)S(1)}, f32[1,4096]{1,0:T(1,128)}, u32[]{:S(2)}) copy-start(f32[1,4096]{1,0:T(1,128)} %slice.363) | copy-start | bytes 49156
  219.8 7.8 %copy-start.8 = (f32[15,4096]{1,0:T(8,128)S(1)}, f32[15,4096]{1,0:T(8,128)}, u32[]{:S(2)}) copy-start(f32[15,4096]{1,0:T(8,128)} %slice.305) | copy-start | bytes 737284
  219.8 7.8 %copy-start.9 = (f32[15,4096]{1,0:T(8,128)S(1)}, f32[15,4096]{1,0:T(8,128)}, u32[]{:S(2)}) copy-start(f32[15,4096]{1,0:T(8,128)} %slice.338) | copy-start | bytes 737284
  225.4 3.9 %copy-start.5 = (f32[31,4096]{1,0:T(8,128)S(1)}, f32[31,4096]{1,0:T(8,128)}, u32[]{:S(2)}) copy-start(f32[31,4096]{1,0:T(8,128)} %slice.299) | copy-start | bytes 1523716
  229.6 11.9 %copy-start.2 = (f32[63,4096]{1,0:T(8,128)S(1)}, f32[63,4096]{1,0:T(8,128)}, u32[]{:S(2)}) copy-start(f32[63,4096]{1,0:T(8,128)} %slice.293) | copy-start | bytes 3096580
  232.9 10.0 %slice-start = ((f32[128,4096]{1,0:T(8,128)}), f32[1,4096]{1,0:T(1,128)S(1)}, s32[]{:S(2)}) async-start(f32[128,4096]{1,0:T(8,128)} %copy-done), calls=%async_computation.2 | async-start | bytes 32768 | tf_op jit(solution)/shard_map/slice | solution.py:132
  242.9 5.0 %copy-start.1 = (f32[128,4096]{1,0:T(8,128)S(1)}, f32[128,4096]{1,0:T(8,128)}, u32[]{:S(2)}) copy-start(f32[128,4096]{1,0:T(8,128)} %pad.156) | copy-start | bytes 6291460
  243.0 6.7 %copy-start.22 = (f32[128]{0:T(128)S(1)}, f32[128]{0:T(128)}, u32[]{:S(2)}) copy-start(f32[128]{0:T(128)} %copy-done.21) | copy-start | bytes 1540
  249.8 13.1 %copy-start.10 = (f32[1024,16]{0,1:T(8,128)S(1)}, f32[1024,16]{0,1:T(8,128)}, u32[]{:S(2)}) copy-start(f32[1024,16]{0,1:T(8,128)} %param.16) | copy-start | bytes 196612
  249.8 13.8 %copy-start.3 = (bf16[1024,1024]{1,0:T(8,128)(2,1)S(1)}, bf16[1024,1024]{1,0:T(8,128)(2,1)}, u32[]{:S(2)}) copy-start(bf16[1024,1024]{1,0:T(8,128)(2,1)} %param.15) | copy-start | bytes 6291460
  251.3 39.0 %all-to-all-start.1 = ((bf16[32,4,4096]{2,1,0:T(4,128)(2,1)}), bf16[32,4,4096]{2,1,0:T(4,128)(2,1)S(1)}, u32[]{:S(2)}, u32[]{:S(2)}) async-start(bf16[32,4,4096]{2,1,0:T(4,128)(2,1)} %all_to_all.30), calls=%async_computation.1 | async-start | bytes 2097152 | tf_op jit(solution)/shard_map/all_to_all | solution.py:137
  259.2 20.1 %collective-permute-start.1 = (bf16[3,128]{1,0:T(4,128)(2,1)}, bf16[3,128]{1,0:T(4,128)(2,1)}, u32[]{:S(2)}, u32[]{:S(2)}) collective-permute-start(bf16[3,128]{1,0:T(4,128)(2,1)} %slice.273), channel_id=1, source_target_pairs={{0,8},{8,16},{16,24},{24,32},{32,40},{40,48},{48,56},{56,64},{64,7... | collective-permute-start | bytes 2312 | tf_op jit(solution)/shard_map/ppermute | solution.py:17
  268.0 8.7 %copy-start.7 = (bf16[1024,1024]{1,0:T(8,128)(2,1)S(1)}, bf16[1024,1024]{1,0:T(8,128)(2,1)}, u32[]{:S(2)}) copy-start(bf16[1024,1024]{1,0:T(8,128)(2,1)} %param.22) | copy-start | bytes 6291460
  275.8 7.2 %copy-start.12 = (f32[4,16,256]{2,1,0:T(8,128)S(1)}, f32[4,16,256]{2,1,0:T(8,128)}, u32[]{:S(2)}) copy-start(f32[4,16,256]{2,1,0:T(8,128)} %copy-done.11) | copy-start | bytes 196612
  (6 other events, 14.2 us)
where the time goes:
time: 333 us; the launch traced here: 330 us
  local copies, waits for them, and re-layouts  129 us (39%)
  blocking collectives  103 us (31%)
  other arithmetic  53.2 us (16%)
  starting transfers between devices  27.5 us (8%)
  matrix products  16.6 us (5%)
    all_gather x1, blocking collectives, shards(): decay_all = lax.all_gather(span_decay, 'seq', axis=0, tiled=True)  77.7 us
    slice x40, local copies, waits for them, and re-layouts, shards(): ending = lax.associative_scan(compose_flat, (factor, spread), axis=0)[1]  67 us
    psum x1, blocking collectives, shards(): lax.psum((jnp.sum(deviation * deviation, axis=1), jnp.sum(roll_float * ro...  25.2 us
    unnamed x54, local copies, waits for them, and re-layouts  15.7 us
    convert_element_type x3, other arithmetic, causal_conv(): return jax.nn.silu(summed).astype(jnp.bfloat16)  15.2 us
    convert_element_type x2, local copies, waits for them, and re-layouts, shards(): gated = mixed * jax.nn.silu(z_trans.astype(jnp.float32))  12.3 us
    ppermute x3, starting transfers between devices, shifted_2(): return lax.ppermute(block, axis, route)  11.6 us
    mul x5, other arithmetic, compose_flat(): return (earlier[0] * later[0], later[0] * earlier[1] + later[1])  11.4 us
  transfers between devices with their start and end apart: 5, of which 0 were waited for; matrix products, arithmetic and copies ran while one was open for 16% of the time, Pallas kernels for 0%

commit v1 on v0

v1 whole, which is shorter than its diff:
```python
import functools

import jax
import jax.numpy as jnp
from jax import lax
from jax.experimental import pallas as pl
from jax.experimental.pallas import tpu as pltpu
from jax.sharding import PartitionSpec as P

HEADS = 128
HEAD_DIM = 64
STATE = 128
GROUPS = 8
CONV_K = 4
SPAN = 256
CHUNK = 128
LANES = 256
HALO = 16

F32 = jnp.float32
BF16 = jnp.bfloat16


def parts3(v):
    hi = v.astype(BF16)
    rest = v - hi.astype(F32)
    mid = rest.astype(BF16)
    low = (rest - mid.astype(F32)).astype(BF16)
    return hi, mid, low


def silu_half(h):
    return h + h * jnp.tanh(h)


def mm(a, b):
    return jnp.dot(a, b, preferred_element_type=F32)


def one_hot(lane0, width=LANES):
    r = lax.broadcasted_iota(jnp.int32, (256, width), 0)
    c = lax.broadcasted_iota(jnp.int32, (256, width), 1)
    return jnp.where((r & 127) == (c + lane0) // HEAD_DIM, 1.0, 0.0).astype(BF16)


def span_keep(seq_ref, span):
    start = seq_ref[0] * 0
    fresh = span == start
    for i in range(seq_ref.shape[0] - 1):
        start = start + seq_ref[i]
        fresh = fresh | (span == start)
    return jnp.where(fresh, 0.0, 1.0).astype(F32)


def conv_block(padded_ref, taps):
    rows = padded_ref.shape[0] - 8
    total = padded_ref[pl.ds(5, rows), :] * taps[0:1]
    for k in range(1, CONV_K):
        total = total + padded_ref[pl.ds(5 + k, rows), :] * taps[k : k + 1]
    return silu_half(total)


def conv_ordered(padded_ref, taps):
    per = CHUNK // 8
    shifted = {m: padded_ref[pl.ds(8 + m, 8, stride=per), :] for m in range(1 - CONV_K, per)}
    rows = []
    for j in range(per):
        total = shifted[j + 1 - CONV_K] * taps[0:1]
        for k in range(1, CONV_K):
            total = total + shifted[j + 1 - CONV_K + k] * taps[k : k + 1]
        rows.append(silu_half(total))
    return jnp.concatenate(rows, axis=0)


def turned(v, heads, chunk):
    turn = (128 - heads * chunk) % 128
    return pltpu.roll(v, turn, 1) if turn else v


def split2(v):
    hi = v.astype(BF16)
    return hi, (v - hi.astype(F32)).astype(BF16)


def stack_scales(source, heads, chunks, target):
    for k in range(chunks):
        hi, low = split2(turned(source, heads, k))
        target[k * CHUNK : (k + 1) * CHUNK, 0:128] = hi
        target[k * CHUNK : (k + 1) * CHUNK, 128:256] = low


def chunk_rates(ts_ref, rate_ref, chunks):
    steps = jnp.concatenate([ts_ref[:, k * CHUNK : (k + 1) * CHUNK] for k in range(chunks)], axis=0).T
    return steps, -steps * jnp.concatenate([rate_ref[...]] * chunks, axis=1)


def sum_rates(picks, rates):
    picks = picks.astype(BF16)
    r1, r2, r3 = parts3(rates)
    return mm(picks, r1) + (mm(picks, r2) + mm(picks, r3))


def spread_rows(v, e):
    n = v.shape[0]
    out = mm(jnp.concatenate(parts3(v), axis=0), e[0:128])
    return out[0:n] + (out[n : 2 * n] + out[2 * n : 3 * n])


def chunk_keeps(chunks, seq_ref, rank_ref):
    per_span = SPAN // CHUNK
    first = rank_ref[0] * (chunks // per_span)
    return [None if k % per_span else span_keep(seq_ref, first + k // per_span) for k in range(chunks)]


def fill_padded(padded_ref, src_ref, edge, k, lanes, keep):
    if k == 0:
        halo = edge
    else:
        halo = src_ref[k * CHUNK - HALO : k * CHUNK, lanes].astype(F32)[HALO - 8 :]
    padded_ref[0:8, :] = halo if keep is None else halo * keep
    padded_ref[8 : 8 + CHUNK, :] = src_ref[k * CHUNK : (k + 1) * CHUNK, lanes].astype(F32)


def tail_kernel(x_ref, b_ref, c_ref, out_ref):
    width = x_ref.shape[1]
    out_ref[:, 0:width] = x_ref[...]
    out_ref[:, width : width + STATE] = b_ref[...]
    out_ref[:, width + STATE : width + 2 * STATE] = c_ref[...]


def state_kernel(
    chunks, seq_ref, rank_ref, x_hbm, b_ref, ts_ref, rate_ref, wx_ref, wb_ref,
    end_ref, head_scale_ref, chain_ref, head_ref,
    x_all, padded, order, lhsu, wide, bt, xs, x_sems,
):
    blocks = x_all.shape[0]
    width = blocks * LANES
    heads = ts_ref.shape[0]

    def x_copy(i):
        lanes = pl.ds(pl.multiple_of(i * LANES, LANES), LANES)
        return pltpu.make_async_copy(x_hbm.at[:, lanes], x_all.at[i], x_sems.at[i])

    def start(i, carry):
        x_copy(i).start()
        return carry

    lax.fori_loop(0, blocks, start, 0)
    steps, rates = chunk_rates(ts_ref, rate_ref, chunks)
    t = lax.broadcasted_iota(jnp.int32, (CHUNK + 16, CHUNK), 0)
    u = lax.broadcasted_iota(jnp.int32, (CHUNK + 16, CHUNK), 1)
    after = sum_rates(jnp.where((u > t) | (t >= CHUNK), 1.0, 0.0), rates)
    totals = after[CHUNK : CHUNK + 16]
    j = lax.broadcasted_iota(jnp.int32, (CHUNK, CHUNK), 0)
    k = lax.broadcasted_iota(jnp.int32, (CHUNK, CHUNK), 1)
    later = jnp.where((lax.rem(j, heads) == lax.rem(k, heads)) & (j > k), 1.0, 0.0).astype(BF16)
    t1, t2, t3 = parts3(totals)
    later = mm(t1, later) + (mm(t2, later) + mm(t3, later))
    lane = lax.broadcasted_iota(jnp.int32, (16, 128), 1)
    reached = jnp.ones((16, 128), F32)
    whole = jnp.exp(later + totals)
    for n in range(0, chunks, SPAN // CHUNK):
        keep = span_keep(seq_ref, rank_ref[0] * (chunks * CHUNK // SPAN) + n * CHUNK // SPAN)
        reached = jnp.where(lane < n * heads, reached * keep, reached)
        whole = whole * keep
    scale = jnp.exp(after[0:CHUNK] + later[0:1]) * steps * reached[0:1]
    order[...] = scale
    per = CHUNK // 8
    stack_scales(jnp.concatenate([order[pl.ds(n, 8, stride=per), :] for n in range(per)], axis=0), heads, chunks, lhsu)
    e = one_hot(0, width)
    wide_all = mm(lhsu[...], e)
    for i in range(blocks):
        wide[i] = wide_all[:, i * LANES : (i + 1) * LANES]
    head_scale_ref[...] = mm(jnp.concatenate(split2(scale[0:HALO]), axis=1), e)
    row = lax.broadcasted_iota(jnp.int32, (16, 1), 0)
    p1, p2, p3 = parts3(whole)
    p = jnp.where(row == 0, p1.astype(F32), jnp.where(row == 1, p2.astype(F32), p3.astype(F32)))
    chain_ref[...] = mm(jnp.where(row < 3, p, 0.0).astype(BF16), e[0:128])[0:8]
    taps = wb_ref[0].astype(F32) * 0.5
    none = jnp.zeros((8, 128), F32)

    keeps = chunk_keeps(chunks, seq_ref, rank_ref)
    for k in range(chunks):
        pad = padded.at[k % 4]
        fill_padded(pad, b_ref, none, k, slice(0, STATE), keeps[k])
        v = conv_ordered(pad, taps)
        if k == 0:
            v = jnp.where((lax.broadcasted_iota(jnp.int32, v.shape, 0) & 7) == 0, 0.0, v)
        bt[:, k * CHUNK : (k + 1) * CHUNK] = v.T.astype(BF16)
    head_ref[:, width : width + STATE] = b_ref[0:HALO, :]

    def block(i, carry):
        lane0 = pl.multiple_of(i * LANES, LANES)
        lanes = pl.ds(lane0, LANES)
        x_ref = x_all.at[i]
        weights = wx_ref[:, lanes].astype(F32) * 0.5
        x_copy(i).wait()
        head_ref[:, lanes] = x_ref[0:HALO, :]

        for k in range(chunks):
            toks = slice(k * CHUNK, (k + 1) * CHUNK)
            for part in range(LANES // 128):
                cols = slice(part * 128, (part + 1) * 128)
                pad = padded.at[(2 * k + part) % 4]
                fill_padded(pad, x_ref, none, k, cols, keeps[k])
                v = conv_ordered(pad, weights[:, cols])
                xs[toks, cols] = (v * wide[i, toks, cols]).astype(BF16)
        end_ref[:, lanes] = mm(bt[...], xs[...])
        return carry

    lax.fori_loop(0, blocks, block, 0)


def edge_kernel(
    chunks, seq_ref, rank_ref, edge_ref, head_ref, wx_ref, wbc_ref, scale_ref, end_ref, chain_ref,
    msg_ref, edge_out_ref,
):
    keep = span_keep(seq_ref, rank_ref[0] * (chunks * CHUNK // SPAN))
    width = wx_ref.shape[1]
    b_cols = slice(width, width + STATE)
    edge_out_ref[...] = edge_ref[...]

    def conv(before, block, taps):
        taps = taps.astype(F32) * 0.5
        joined = jnp.concatenate([before.astype(F32)[HALO - 8 :] * keep, block.astype(F32)], axis=0)
        total = joined[5 : 5 + HALO] * taps[0:1]
        for k in range(1, CONV_K):
            total = total + joined[5 + k : 5 + k + HALO] * taps[k : k + 1]
        return silu_half(total)

    bc = conv(edge_ref[:, b_cols], head_ref[:, b_cols], wbc_ref[0])
    bt = jnp.concatenate([bc, jnp.zeros((STATE - HALO, STATE), F32)], axis=0).T[:, 0:HALO].astype(BF16)

    for i in range(width // LANES):
        cols = slice(i * LANES, (i + 1) * LANES)
        v = conv(edge_ref[:, cols], head_ref[:, cols], wx_ref[:, cols])
        xs = (v * scale_ref[:, cols]).astype(BF16)
        state = end_ref[:, cols] + mm(bt, xs)
        both = jnp.concatenate([state, chain_ref[:, cols]], axis=0)
        for part in range(LANES // 128):
            piece = both[:, part * 128 : (part + 1) * 128]
            for nb in range(4):
                own = jnp.concatenate([piece[nb * 32 : (nb + 1) * 32], piece[STATE:]], axis=0)
                msg_ref[(i * (LANES // 128) + part) * 4 + nb] = own.astype(BF16)


def scan_kernel(in_ref, after_ref, out_ref):
    def some(m, carried):
        for n in range(8):
            i = 8 * m + n
            out_ref[i] = carried.astype(BF16)
            block = in_ref[i].astype(F32)
            decay = block[32:33] + (block[33:34] + block[34:35])
            carried = carried * decay + block[0:32]
        return carried

    lax.fori_loop(0, in_ref.shape[0] // 8, some, jnp.zeros((32, 128), F32))


def mix_first(chunks, seq_ref, rank_ref, b_ref, c_ref, edge_ref, wbc_ref, left, bt, cc_ref, padded):
    t = lax.broadcasted_iota(jnp.int32, (CHUNK, CHUNK), 0)
    u = lax.broadcasted_iota(jnp.int32, (CHUNK, CHUNK), 1)
    edges = edge_ref[...].astype(F32)[HALO - 8 :]

    keeps = chunk_keeps(chunks, seq_ref, rank_ref)
    for k in range(chunks):
        toks = slice(k * CHUNK, (k + 1) * CHUNK)
        pair = []
        for i, ref in enumerate((b_ref, c_ref)):
            pad = padded.at[(2 * k + i) % 4]
            fill_padded(pad, ref, edges[:, i * STATE : (i + 1) * STATE], k, slice(0, STATE), keeps[k])
            pair.append(conv_block(pad, wbc_ref[i].astype(F32) * 0.5))
        b, c = pair
        bt[k] = b.T.astype(BF16)
        c = c.astype(BF16)
        cc_ref[toks, :] = c
        left[toks, 128:256] = c
        g = lax.dot_general(c, b.astype(BF16), (((1,), (1,)), ((), ())), preferred_element_type=F32)
        left[toks, 0:128] = jnp.where(u <= t, g, 0.0).astype(BF16)


def mix_kernel(
    chunks, lane_first, seq_ref, rank_ref, x_ref, edge_ref, ts_ref, rate_ref, z_ref, roll_ref, wx_ref, skip_ref, *refs
):
    if lane_first == 0:
        b_ref, c_ref, bc_edge_ref, wbc_ref, a_ref, f_ref, roll_sum_ref, left, bt, cc_ref = refs[:10]
    else:
        left, bt, a_ref, f_ref, roll_sum_ref = refs[:5]
    padded, wide_u, wide_t, part, state, lhsu, lhst, ends_all, rows = refs[-9:]
    heads = skip_ref.shape[1]

    @pl.when(pl.program_id(0) == 0)
    def _():
        if lane_first == 0:
            mix_first(chunks, seq_ref, rank_ref, b_ref, c_ref, bc_edge_ref, wbc_ref, left, bt, cc_ref, padded)
        steps, rates = chunk_rates(ts_ref, rate_ref, chunks)
        t = lax.broadcasted_iota(jnp.int32, (CHUNK + 16, CHUNK), 0)
        u = lax.broadcasted_iota(jnp.int32, (CHUNK + 16, CHUNK), 1)
        half = jnp.where(u < CHUNK // 2, 1.0, 0.0)
        tri = jnp.where(u <= t, 1.0, 0.0) - half
        cum = sum_rates(jnp.where(t < CHUNK, tri, jnp.where(t == CHUNK, half, 1.0)), rates)
        rel = cum[:CHUNK]
        stack_scales(jnp.exp(-rel) * steps, heads, chunks, lhsu)
        stack_scales(jnp.exp(rel), heads, chunks, lhst)
        ends = jnp.exp(jnp.concatenate([rel[CHUNK - 8 :], cum[CHUNK : CHUNK + 8]], axis=0))
        for k in range(chunks):
            ends_all[k] = turned(ends, heads, k)
        part[...] = jnp.zeros_like(part)

    e = one_hot(lane_first + pl.program_id(0) * LANES)
    rows[...] = spread_rows(ends_all[...].reshape(16 * chunks, 128), e).reshape(chunks, 16, LANES)
    wide_u[...] = mm(lhsu[...], e)
    wide_t[...] = mm(lhst[...], e)
    s1, s2, s3 = parts3(skip_ref[...])
    skip = mm(jnp.concatenate([s1.astype(F32), s2.astype(F32), s3.astype(F32)], axis=0).astype(BF16), e[0:heads])
    skip = skip[0:1] + (skip[1:2] + skip[2:3])
    state[...] = jnp.zeros_like(state)
    edges = edge_ref[...].astype(F32)[HALO - 8 :]
    weights = wx_ref[...].astype(F32) * 0.5

    keeps = chunk_keeps(chunks, seq_ref, rank_ref)
    reach = jnp.ones((1, LANES), F32)
    for k in range(chunks):
        toks = slice(k * CHUNK, (k + 1) * CHUNK)
        to_end, to_mid, whole = rows[k, 7:8, :], rows[k, 8:9, :], rows[k, 9:10, :]
        xs, direct = [], []
        for lane in range(0, LANES, 128):
            cols = slice(lane, lane + 128)
            pad = padded.at[(2 * k + lane // 128) % 4]
            fill_padded(pad, x_ref, edges[:, cols], k, cols, keeps[k])
            v = conv_block(pad, weights[:, cols])
            xs.append((v * wide_u[toks, cols]).astype(BF16))
            direct.append(v.astype(BF16).astype(F32) * skip[:, cols])
        xs, direct = jnp.concatenate(xs, axis=1), jnp.concatenate(direct, axis=1)
        before = state[...]
        if keeps[k] is not None:
            before = before * keeps[k]
            reach = reach * keeps[k]
        state[...] = before * whole + mm(bt[k], xs) * to_end
        right = jnp.concatenate([xs, (before * to_mid).astype(BF16)], axis=0)
        inner = mm(left[toks, :], right)
        scale = wide_t[toks, :]
        gate = silu_half(z_ref[toks, :].astype(F32) * 0.5)
        a_ref[toks, :] = ((inner * scale + direct) * gate).astype(BF16)
        f_ref[toks, :] = (scale * gate * (reach * to_mid)).astype(BF16)
        r = roll_ref[toks, :].astype(F32)
        r = r * r
        part[toks, :] += r[:, 0:128] + r[:, 128:256]
        reach = reach * whole

    @pl.when(pl.program_id(0) == pl.num_programs(0) - 1)
    def _():
        for k in range(chunks):
            roll_sum_ref[k : k + 1, :] = jnp.sum(part[k * CHUNK : (k + 1) * CHUNK, :].T, axis=0, keepdims=True)


def norm_kernel(
    in_ref, a1_all, f1_all, cc_hbm, a0_hbm, f0_hbm, roll_hbm, gain_hbm, roll0_hbm, roll1_hbm, out_hbm, sums_ref,
    entering, gated, a0_all, f0_all, roll_all, out_all, cc_ref, gain_ref, roll0_ref, roll1_ref, sums,
    in_sems, out_sems, small_sems,
):
    width = out_all.shape[1]
    chunks, half = out_all.shape[0] // CHUNK, a0_all.shape[1]
    pairs = [(cc_hbm, cc_ref), (a0_hbm, a0_all), (f0_hbm, f0_all), (roll_hbm, roll_all)]
    smalls = [(gain_hbm, gain_ref), (roll0_hbm, roll0_ref), (roll1_hbm, roll1_ref)]
    size = 2 * CHUNK

    def copy_in(i, m):
        here = pl.ds(pl.multiple_of(m * size, size), size)
        return pltpu.make_async_copy(pairs[i][0].at[here], pairs[i][1].at[here], in_sems.at[i, m])

    def copy_out(m):
        here = pl.ds(pl.multiple_of(m * size, size), size)
        return pltpu.make_async_copy(out_all.at[here], out_hbm.at[here], out_sems.at[m])

    def copy_small(i):
        return pltpu.make_async_copy(*smalls[i], small_sems.at[i])

    for m in range(chunks // 2):
        for i in range(len(pairs)):
            copy_in(i, m).start()
        if m == 0:
            for i in range(len(smalls)):
                copy_small(i).start()
    for lb in range(width // 128):
        for nb in range(4):
            entering[nb * 32 : (nb + 1) * 32, lb * 128 : (lb + 1) * 128] = in_ref[lb * 4 + nb]
    for i in range(len(smalls)):
        copy_small(i).wait()

    def two(m, carry):
        for i in range(len(pairs)):
            copy_in(i, m).wait()
        scales = []
        for n in range(2):
            toks = pl.ds(pl.multiple_of(m * size + n * CHUNK, CHUNK), CHUNK)
            squares = jnp.zeros((CHUNK, 128), F32)
            for lane in range(0, width, LANES):
                cols = slice(lane, lane + LANES)
                a_ref, f_ref = (a0_all, f0_all) if lane < half else (a1_all, f1_all)
                own = slice(lane % half, lane % half + LANES)
                g = a_ref[toks, own].astype(F32) + f_ref[toks, own].astype(F32) * mm(cc_ref[toks, :], entering[:, cols])
                gated[n, :, cols] = g
                g = g * g
                squares = squares + (g[:, 0:128] + g[:, 128:256])
            mean = jnp.sum(squares, axis=1, keepdims=True) * (1.0 / width)
            scales.append(lax.rsqrt(mean + 1e-05))
        for n in range(2):
            toks = pl.ds(pl.multiple_of(m * size + n * CHUNK, CHUNK), CHUNK)
            squares = jnp.zeros((CHUNK, 128), F32)
            for lane in range(0, width, 128):
                cols = slice(lane, lane + 128)
                v = (gated[n, :, cols] * scales[n] * gain_ref[:, cols]).astype(BF16)
                out_all[toks, cols] = v
                d = v.astype(F32) - roll_all[toks, cols].astype(F32)
                squares = squares + d * d
            sums[pl.ds(2 * m + n, 1), :] = jnp.sum(squares.T, axis=0, keepdims=True)
        copy_out(m).start()
        return carry

    lax.fori_loop(0, chunks // 2, two, 0)
    both = jnp.concatenate([sums[...], roll0_ref[...] + roll1_ref[...]], axis=0)
    for i in range(sums_ref.shape[0]):
        sums_ref[i] = both
    for m in range(chunks // 2):
        copy_out(m).wait()


def shards(
    x_values, b_values, c_values, z_values, time_steps, decay_rate, skip_gain,
    conv_x, conv_bc, norm_gain, rollout, seq_spans,
):
    ring = lax.axis_size("seq")
    rows, width = x_values.shape
    heads = decay_rate.shape[0]
    chunks = rows // CHUNK
    blocks = width // LANES
    rank = lax.axis_index("seq").astype(jnp.int32).reshape(1)

    ends = width + 2 * STATE
    smem = pl.BlockSpec(memory_space=pltpu.SMEM)

    def whole(*shape):
        return pl.BlockSpec(shape, lambda i: (0,) * len(shape))

    def lane_block(r, first=0):
        return pl.BlockSpec((r, LANES), lambda i: (0, first + i))

    def grant(mib):
        return pltpu.CompilerParams(vmem_limit_bytes=mib * 1024 * 1024)

    def in_hbm(*arrays):
        return [pltpu.with_memory_space_constraint(v, pltpu.HBM) for v in arrays]

    x_values, b_values, c_values, z_values, rollout = in_hbm(x_values, b_values, c_values, z_values, rollout)
    (seq_spans,) = in_hbm(seq_spans)
    steps_row, rate_row, skip_row, gain_row, conv_x, conv_bc = in_hbm(
        time_steps.T, decay_rate.reshape(1, heads), skip_gain.reshape(1, heads), norm_gain.reshape(1, width), conv_x, conv_bc
    )
    last = rows // HALO - 1
    edge = pl.pallas_call(
        tail_kernel,
        grid=(1,),
        in_specs=[pl.BlockSpec((HALO, n), lambda i: (last, 0)) for n in (width, STATE, STATE)],
        out_specs=whole(HALO, ends),
        out_shape=jax.ShapeDtypeStruct((HALO, ends), BF16),
        compiler_params=grant(8),
        name="tails",
    )(x_values, b_values, c_values)
    edge = lax.ppermute(edge, "seq", [(i, i + 1) for i in range(ring - 1)])
    conv_scratch = pltpu.VMEM((4, 8 + CHUNK, 128), F32)
    wide_scratch = pltpu.VMEM((rows, LANES), F32)

    vmem = pl.BlockSpec(memory_space=pltpu.VMEM)
    hbm = pl.BlockSpec(memory_space=pl.ANY)
    end, head_scale, chain, head = pl.pallas_call(
        functools.partial(state_kernel, chunks),
        in_specs=[smem, smem, hbm] + [vmem] * 5,
        out_specs=[vmem] * 4,
        out_shape=[
            jax.ShapeDtypeStruct((STATE, width), F32),
            jax.ShapeDtypeStruct((HALO, width), F32),
            jax.ShapeDtypeStruct((8, width), F32),
            jax.ShapeDtypeStruct((HALO, width + STATE), BF16),
        ],
        scratch_shapes=[
            pltpu.VMEM((blocks, rows, LANES), BF16),
            conv_scratch,
            pltpu.VMEM((CHUNK, 128), F32),
            pltpu.VMEM((rows, 256), BF16),
            pltpu.VMEM((blocks, rows, LANES), F32),
            pltpu.VMEM((STATE, rows), BF16),
            pltpu.VMEM((rows, LANES), BF16),
            pltpu.SemaphoreType.DMA((blocks,)),
        ],
        compiler_params=grant(16),
        cost_estimate=pl.CostEstimate(flops=1 << 29, bytes_accessed=4 << 20, transcendentals=1 << 20),
        name="states",
    )(seq_spans, rank, x_values, b_values, steps_row, rate_row, conv_x, conv_bc)

    msg, edge = pl.pallas_call(
        functools.partial(edge_kernel, chunks),
        grid=(1,),
        in_specs=[
            smem, smem, whole(HALO, ends), whole(HALO, width + STATE), whole(CONV_K, width),
            whole(2, CONV_K, STATE), whole(HALO, width), whole(STATE, width), whole(8, width),
        ],
        out_specs=[whole(ring, 40, 128), whole(HALO, ends)],
        out_shape=[jax.ShapeDtypeStruct((ring, 40, 128), BF16), pltpu.HBM((HALO, ends), BF16)],
        compiler_params=grant(8),
        name="edge_states",
    )(seq_spans, rank, edge, head, conv_x, conv_bc, head_scale, end, chain)
    (edge,) = in_hbm(edge)

    spread = lax.all_to_all(msg, "seq", split_axis=0, concat_axis=0, tiled=True)

    def mix(first, specs, operands, more_specs, more_shapes):
        half = blocks // 2
        place = pltpu.HBM if first == 0 else pltpu.VMEM
        return pl.pallas_call(
            functools.partial(mix_kernel, chunks, first * LANES),
            grid=(half,),
            in_specs=[
                smem, smem, lane_block(rows, first), lane_block(HALO, first), whole(heads, rows), whole(1, heads),
                lane_block(rows, first), lane_block(rows, first), lane_block(CONV_K, first), whole(1, heads),
            ]
            + specs,
            out_specs=[lane_block(rows), lane_block(rows), whole(chunks, CHUNK)] + more_specs,
            out_shape=[
                place((rows, half * LANES), BF16),
                place((rows, half * LANES), BF16),
                pltpu.HBM((chunks, CHUNK), F32),
            ]
            + more_shapes,
            scratch_shapes=[
                conv_scratch, wide_scratch, wide_scratch, pltpu.VMEM((rows, 128), F32), pltpu.VMEM((STATE, LANES), F32),
                pltpu.VMEM((rows, 256), BF16), pltpu.VMEM((rows, 256), BF16), pltpu.VMEM((chunks, 16, 128), F32),
                pltpu.VMEM((chunks, 16, LANES), F32),
            ],
            compiler_params=grant(32),
            cost_estimate=pl.CostEstimate(flops=1 << 30, bytes_accessed=9 << 20, transcendentals=1 << 20),
            name="mix_first" if first == 0 else "mix_second",
        )(
            seq_spans, rank, x_values, edge, steps_row, rate_row, z_values, rollout, conv_x,
            skip_row, *operands,
        )

    shared_specs = [whole(rows, 256), whole(chunks, STATE, CHUNK)]
    a0, f0, roll0, left, bt, cc = mix(
        0,
        [
            whole(rows, STATE), whole(rows, STATE), pl.BlockSpec((HALO, 2 * STATE), lambda i: (0, width // (2 * STATE))),
            whole(2, CONV_K, STATE),
        ],
        [b_values, c_values, edge, conv_bc],
        shared_specs + [whole(rows, STATE)],
        [
            pltpu.HBM((rows, 256), BF16),
            pltpu.HBM((chunks, STATE, CHUNK), BF16),
            pltpu.HBM((rows, STATE), BF16),
        ],
    )
    a0, f0, roll0, left, bt, cc = in_hbm(a0, f0, roll0, left, bt, cc)
    a1, f1, roll1 = mix(blocks // 2, shared_specs, [left, bt], [], [])
    a1, f1 = (pltpu.with_memory_space_constraint(v, pltpu.VMEM) for v in (a1, f1))
    (roll1,) = in_hbm(roll1)

    entering = pl.pallas_call(
        scan_kernel,
        in_specs=[pl.BlockSpec(memory_space=pltpu.VMEM), pl.BlockSpec(memory_space=pl.ANY)],
        out_shape=jax.ShapeDtypeStruct((ring, 32, 128), BF16),
        compiler_params=grant(8),
        name="scan",
    )(spread, roll0)
    entering = lax.all_to_all(entering, "seq", split_axis=0, concat_axis=0, tiled=True)

    group = lax.axis_size("head")
    normed, sums = pl.pallas_call(
        norm_kernel,
        in_specs=[vmem] * 3 + [hbm] * 7,
        out_specs=[hbm, vmem],
        out_shape=[pltpu.HBM((rows, width), BF16), jax.ShapeDtypeStruct((group, 2 * chunks, CHUNK), F32)],
        scratch_shapes=[pltpu.VMEM((STATE, width), BF16), pltpu.VMEM((2, CHUNK, width), F32)]
        + [pltpu.VMEM((rows, width // 2), BF16)] * 2
        + [pltpu.VMEM((rows, width), BF16)] * 2
        + [pltpu.VMEM((rows, STATE), BF16), pltpu.VMEM((1, width), F32)]
        + [pltpu.VMEM((chunks, CHUNK), F32)] * 3
        + [pltpu.SemaphoreType.DMA((n, chunks // 2)) for n in (4,)]
        + [pltpu.SemaphoreType.DMA((chunks // 2,)), pltpu.SemaphoreType.DMA((3,))],
        compiler_params=grant(24),
        cost_estimate=pl.CostEstimate(flops=1 << 28, bytes_accessed=8 << 20, transcendentals=1 << 10),
        name="norms",
    )(entering, a1, f1, cc, a0, f0, rollout, gain_row, roll0, roll1)

    sums = jnp.sum(lax.all_to_all(sums, "head", split_axis=0, concat_axis=0, tiled=True), axis=0)
    relative = jnp.sqrt(sums[:chunks] / (sums[chunks:] + 1e-06))
    return normed, relative.reshape(rows)


def solution(mesh):
    placed = (
        P("seq", "head"), P("seq", "head"), P("seq", "head"), P("seq", "head"), P("seq", "head"),
        P("head"), P("head"), P(None, "head"), P(None, None, "head"), P("head"), P("seq", "head"), P(),
    )
    return jax.shard_map(
        shards, mesh=mesh, in_specs=placed, out_specs=(P("seq", "head"), P("seq")), check_vma=False
    )
```

time: 333 us -> 71.6 us (0.22)
  local copies, waits for them, and re-layouts: 129 us -> 0 us
  blocking collectives: 103 us -> 12.9 us
  other arithmetic: 53.2 us -> 0.62 us
  Pallas kernels: 0 us -> 30 us
  matrix products: 16.6 us -> 0 us
  starting transfers between devices: 27.5 us -> 21.6 us
  waiting for transfers between devices: 0.01 us -> 5.36 us
    all_gather x1 -> x0, blocking collectives: 77.7 us -> none  [shards(): decay_all = lax.all_gather(span_decay, 'seq', axis=0, tiled=True)]
    slice x47 -> x0, local copies, waits for them, and re-layouts: 74.9 us -> none  [the longest x40 67 us: shards(): ending = lax.associative_scan(compose_flat, (factor, spread), axis=0)[1]]
    pallas_call x0 -> x7, Pallas kernels: none -> 30 us  [the longest x2 14.3 us: mix(): pl.pallas_call(functools.partial(mix_kernel, chunks, first * LANES), grid...]
    psum x1 -> x0, blocking collectives: 25.2 us -> none  [shards(): lax.psum((jnp.sum(deviation * deviation, axis=1), jnp.sum(roll_float * ro...]
    convert_element_type x6 -> x0, other arithmetic: 17 us -> none  [the longest x3 15.2 us: causal_conv(): return jax.nn.silu(summed).astype(jnp.bfloat16)]
    dot_general x5 -> x0, matrix products: 16.6 us -> none  [the longest x1 7.28 us: shards(): jnp.einsum('sgqpu,sgqtu->sgqpt', x_trans, mixing, preferred_element_type=...]
    unnamed x54 -> x0, local copies, waits for them, and re-layouts: 15.7 us -> none
    all_to_all x0 -> x1, blocking collectives: none -> 12.9 us  [shards(): lax.all_to_all(sums, 'head', split_axis=0, concat_axis=0, tiled=True)]
  transfers between devices with their start and end apart: 5 -> 3, of which waited for: 0 -> 2; matrix products, arithmetic and copies ran while one was open for 16% -> 0% of each run, Pallas kernels for 0% -> 29%
where the time goes in v1:
time: 71.6 us; the launch traced here: 71.1 us
  Pallas kernels  30 us (42%)
  starting transfers between devices  21.6 us (30%)
  blocking collectives  12.9 us (18%)
  waiting for transfers between devices  5.36 us (7%)
    pallas_call x2, Pallas kernels, mix(): pl.pallas_call(functools.partial(mix_kernel, chunks, first * LANES), grid...  14.3 us
    all_to_all x1, blocking collectives, shards(): lax.all_to_all(sums, 'head', split_axis=0, concat_axis=0, tiled=True)  12.9 us
    all_to_all x1, starting transfers between devices, shards(): spread = lax.all_to_all(msg, 'seq', split_axis=0, concat_axis=0, tiled=True)  10.1 us
    all_to_all x1, starting transfers between devices, shards(): lax.all_to_all(entering, 'seq', split_axis=0, concat_axis=0, tiled=True)  7.09 us
    pallas_call x1, Pallas kernels, shards(): pl.pallas_call(functools.partial(state_kernel, chunks), in_specs=[smem, s...  6.65 us
    pallas_call x1, Pallas kernels, shards(): pl.pallas_call(norm_kernel, in_specs=[vmem] * 3 + [hbm] * 7, out_specs=[h...  5.74 us
    ppermute x1, starting transfers between devices, shards(): edge = lax.ppermute(edge, 'seq', [(i, i + 1) for i in range(ring - 1)])  4.36 us
    all_to_all x1, waiting for transfers between devices, shards(): lax.all_to_all(entering, 'seq', split_axis=0, concat_axis=0, tiled=True)  3.05 us
  transfers between devices with their start and end apart: 3, of which 2 were waited for; matrix products, arithmetic and copies ran while one was open for 0% of the time, Pallas kernels for 29%

profile of v1, /device:TPU:1, one launch (start us, length us, event | category | flops | bytes accessed | tf_op | source)
XLA Modules:
  0.0 71.1 jit_solution(14163080693387364735)
XLA Ops:
  0.6 0.8 %tails.1 = bf16[16,1280]{1,0:T(8,128)(2,1)S(1)} custom-call(bf16[1024,1024]{1,0:T(8,128)(2,1)} %x_ref.5, bf16[1024,128]{1,0:T(8,128)(2,1)} %refs_0_.1, bf16[1024,128]{1,0:T(8,128)(2,1)} %refs_1_.1), custom_call_target="tpu_custom_call" | custom-call | tf_op jit(solution)/shard_map/tails/pallas_call | solution.py:461
  1.4 4.4 %collective-permute-start = (bf16[16,1280]{1,0:T(8,128)(2,1)S(1)}, bf16[16,1280]{1,0:T(8,128)(2,1)S(1)}, u32[]{:S(2)}, u32[]{:S(2)}) collective-permute-start(bf16[16,1280]{1,0:T(8,128)(2,1)S(1)} %tails.1), channel_id=1, source_target_pairs={{0,8},{8,16},{16,24},{24,32},{32,40},{40,48},{48,56},{56,64},{64,7... | collective-permute-start | bytes 122888 | tf_op jit(solution)/shard_map/ppermute | solution.py:470
  5.8 6.7 %states.1 = (f32[128,1024]{1,0:T(8,128)S(1)}, f32[16,1024]{1,0:T(8,128)S(1)}, f32[8,1024]{1,0:T(8,128)S(1)}, bf16[16,1152]{1,0:T(8,128)(2,1)S(1)}) custom-call(s32[4]{0:T(128)} %seq_ref.7, s32[1]{0:T(128)} %bitcast.rank_ref, bf16[1024,1024]{1,0:T(8,128)(2,1)} %x_ref.5, bf16[1024,128]{1,0:T(8,128)(2,1)} %refs_0_.1, f32[16,1024]{1,0:T(8,128)} %bitcast.7, ...), custom_call_target="tpu_custom_call" | custom-call | flops 536870912 | bytes 4194304 | tf_op jit(solution)/shard_map/states/pallas_call | solution.py:476
  12.4 0.0 collective-permute-done.edge_ref
  12.5 1.7 %edge_states.1 = (bf16[32,40,128]{2,1,0:T(8,128)(2,1)}, bf16[16,1280]{1,0:T(8,128)(2,1)}) custom-call(s32[4]{0:T(128)} %seq_ref.7, s32[1]{0:T(128)} %bitcast.rank_ref, bf16[16,1280]{1,0:T(8,128)(2,1)S(1)} %collective-permute-done.edge_ref, bf16[16,1152]{1,0:T(8,128)(2,1)S(1)} %get-tuple-element.19.head_ref, bf16[4,1024]{1,0:T(4,128)(2,1)} %wx_ref.7, ...), custom_call_target="tpu_custom_call" | custom-call | tf_op jit(solution)/shard_map/edge_states/pallas_call | solution.py:501
  14.2 10.1 %all-to-all-start = ((bf16[32,40,128]{2,1,0:T(8,128)(2,1)}), bf16[32,40,128]{2,1,0:T(8,128)(2,1)S(1)}, u32[]{:S(2)}, u32[]{:S(2)}) async-start(bf16[32,40,128]{2,1,0:T(8,128)(2,1)} %get-tuple-element.23), calls=%async_computation | async-start | bytes 655360 | tf_op jit(solution)/shard_map/all_to_all | solution.py:515
  24.3 7.6 %mix_first.1 = (bf16[1024,512]{1,0:T(8,128)(2,1)}, bf16[1024,512]{1,0:T(8,128)(2,1)}, f32[8,128]{1,0:T(8,128)}, bf16[1024,256]{1,0:T(8,128)(2,1)}, bf16[8,128,12...) custom-call(s32[4]{0:T(128)} %seq_ref.7, s32[1]{0:T(128)} %bitcast.rank_ref, bf16[1024,1024]{1,0:T(8,128)(2,1)} %x_ref.5, ...), custom_call_target="tpu_custom_call" | custom-call | flops 1073741824 | bytes 9437184 | tf_op jit(solution)/shard_map/mix_first/pallas_call | solution.py:520
  32.0 2.3 %all-to-all-done.in_ref = bf16[32,40,128]{2,1,0:T(8,128)(2,1)S(1)} async-done(((bf16[32,40,128]{2,1,0:T(8,128)(2,1)}), bf16[32,40,128]{2,1,0:T(8,128)(2,1)S(1)}, u32[]{:S(2)}, u32[]{:S(2)}) %all-to-all-start) | async-done | bytes 327712 | tf_op jit(solution)/shard_map/all_to_all | solution.py:515
  34.3 0.8 %scan.1 = bf16[32,32,128]{2,1,0:T(8,128)(2,1)} custom-call(bf16[32,40,128]{2,1,0:T(8,128)(2,1)S(1)} %all-to-all-done.in_ref, f32[8,128]{1,0:T(8,128)} %get-tuple-element.25.after_ref.roll0_hbm), custom_call_target="tpu_custom_call" | custom-call | tf_op jit(solution)/shard_map/scan/pallas_call | solution.py:568
  35.1 7.1 %all-to-all-start.1 = ((bf16[32,32,128]{2,1,0:T(8,128)(2,1)}), bf16[32,32,128]{2,1,0:T(8,128)(2,1)S(1)}, u32[]{:S(2)}, u32[]{:S(2)}) async-start(bf16[32,32,128]{2,1,0:T(8,128)(2,1)} %scan.1), calls=%async_computation.1 | async-start | bytes 524288 | tf_op jit(solution)/shard_map/all_to_all | solution.py:575
  42.2 6.6 %mix_second.1 = (bf16[1024,512]{1,0:T(8,128)(2,1)S(1)}, bf16[1024,512]{1,0:T(8,128)(2,1)S(1)}, f32[8,128]{1,0:T(8,128)}) custom-call(s32[4]{0:T(128)} %seq_ref.7, s32[1]{0:T(128)} %bitcast.rank_ref, bf16[1024,1024]{1,0:T(8,128)(2,1)} %x_ref.5, bf16[16,1280]{1,0:T(8,128)(2,1)} %get-tuple-element.24.edge_ref.refs_2_, f32[16,1024]{1,0:T(8,128)} %bitcast.9, ...), custom_call_target="tpu_custom_call" | custom-call | flops 1073741824 | bytes 9437184 | tf_op jit(solution)/shard_map/mix_second/pallas_call | solution.py:520
  48.8 3.0 %all-to-all-done.1.in_ref = bf16[32,32,128]{2,1,0:T(8,128)(2,1)S(1)} async-done(((bf16[32,32,128]{2,1,0:T(8,128)(2,1)}), bf16[32,32,128]{2,1,0:T(8,128)(2,1)S(1)}, u32[]{:S(2)}, u32[]{:S(2)}) %all-to-all-start.1) | async-done | bytes 262176 | tf_op jit(solution)/shard_map/all_to_all | solution.py:575
  51.9 5.7 %norms.1 = (bf16[1024,1024]{1,0:T(8,128)(2,1)}, f32[8,16,128]{2,1,0:T(8,128)S(1)}) custom-call(bf16[32,32,128]{2,1,0:T(8,128)(2,1)S(1)} %all-to-all-done.1.in_ref, bf16[1024,512]{1,0:T(8,128)(2,1)S(1)} %get-tuple-element.28.a1_all, bf16[1024,512]{1,0:T(8,128)(2,1)S(1)} %get-tuple-element.29.f1_all, bf16[1024,128]{1,0:T(8,128)(2,1)} %get-tuple-element.30.cc_hbm, ...), custom_call_target="tpu_custom_call" | custom-call | flops 268435456 | bytes 8388608 | tf_op jit(solution)/shard_map/norms/pallas_call | solution.py:578
  57.6 12.9 %all_to_all.15 = f32[8,16,128]{2,1,0:T(8,128)S(1)} all-to-all(f32[8,16,128]{2,1,0:T(8,128)S(1)} %get-tuple-element.35), channel_id=1, replica_groups=mesh['seq'=32,'head'=8] {'head'}, dimensions={0} | all-to-all | bytes 131072 | tf_op jit(solution)/shard_map/all_to_all | solution.py:595
  70.5 0.6 fusion.2
  (1 shorter events, 0.0 us)
Async XLA Ops:
  1.4 11.0 %collective-permute-start = (bf16[16,1280]{1,0:T(8,128)(2,1)S(1)}, bf16[16,1280]{1,0:T(8,128)(2,1)S(1)}, u32[]{:S(2)}, u32[]{:S(2)}) collective-permute-start(bf16[16,1280]{1,0:T(8,128)(2,1)S(1)} %tails.1), channel_id=1, source_target_pairs={{0,8},{8,16},{16,24},{24,32},{32,40},{40,48},{48,56},{56,64},{64,7... | collective-permute-start | bytes 122888 | tf_op jit(solution)/shard_map/ppermute | solution.py:470
  14.2 20.1 %all-to-all-start = ((bf16[32,40,128]{2,1,0:T(8,128)(2,1)}), bf16[32,40,128]{2,1,0:T(8,128)(2,1)S(1)}, u32[]{:S(2)}, u32[]{:S(2)}) async-start(bf16[32,40,128]{2,1,0:T(8,128)(2,1)} %get-tuple-element.23), calls=%async_computation | async-start | bytes 655360 | tf_op jit(solution)/shard_map/all_to_all | solution.py:515
  35.1 16.8 %all-to-all-start.1 = ((bf16[32,32,128]{2,1,0:T(8,128)(2,1)}), bf16[32,32,128]{2,1,0:T(8,128)(2,1)S(1)}, u32[]{:S(2)}, u32[]{:S(2)}) async-start(bf16[32,32,128]{2,1,0:T(8,128)(2,1)} %scan.1), calls=%async_computation.1 | async-start | bytes 524288 | tf_op jit(solution)/shard_map/all_to_all | solution.py:575

commit v2 on v1

--- a/solution.py
+++ b/solution.py
@@ -130,7 +130,7 @@
 
 def state_kernel(
     chunks, seq_ref, rank_ref, x_hbm, b_ref, ts_ref, rate_ref, wx_ref, wb_ref,
-    end_ref, head_scale_ref, chain_ref, head_ref,
+    end_ref, head_scale_ref, chain_ref, head_ref, taps_ref,
     x_all, padded, order, lhsu, wide, bt, xs, x_sems,
 ):
     blocks = x_all.shape[0]
@@ -188,6 +188,9 @@
             v = jnp.where((lax.broadcasted_iota(jnp.int32, v.shape, 0) & 7) == 0, 0.0, v)
         bt[:, k * CHUNK : (k + 1) * CHUNK] = v.T.astype(BF16)
     head_ref[:, width : width + STATE] = b_ref[0:HALO, :]
+    taps_ref[0:CONV_K, 0:width] = wx_ref[...].astype(F32) * 0.5
+    taps_ref[0:CONV_K, width : width + STATE] = taps
+    taps_ref[CONV_K : CONV_K + 1, :] = jnp.ones((1, width + STATE), F32) * keeps[0]
 
     def block(i, carry):
         lane0 = pl.multiple_of(i * LANES, LANES)
@@ -204,36 +207,33 @@
                 pad = padded.at[(2 * k + part) % 4]
                 fill_padded(pad, x_ref, none, k, cols, keeps[k])
                 v = conv_ordered(pad, weights[:, cols])
-                xs[toks, cols] = (v * wide[i, toks, cols]).astype(BF16)
-        end_ref[:, lanes] = mm(bt[...], xs[...])
+                xs[i, toks, cols] = (v * wide[i, toks, cols]).astype(BF16)
         return carry
 
     lax.fori_loop(0, blocks, block, 0)
-
-
-def edge_kernel(
-    chunks, seq_ref, rank_ref, edge_ref, head_ref, wx_ref, wbc_ref, scale_ref, end_ref, chain_ref,
-    msg_ref, edge_out_ref,
-):
-    keep = span_keep(seq_ref, rank_ref[0] * (chunks * CHUNK // SPAN))
-    width = wx_ref.shape[1]
+    for i in range(blocks):
+        end_ref[:, i * LANES : (i + 1) * LANES] = mm(bt[...], xs[i])
+
+
+def edge_kernel(edge_ref, head_ref, taps_ref, scale_ref, end_ref, chain_ref, msg_ref):
+    width = end_ref.shape[1]
     b_cols = slice(width, width + STATE)
-    edge_out_ref[...] = edge_ref[...]
-
-    def conv(before, block, taps):
-        taps = taps.astype(F32) * 0.5
-        joined = jnp.concatenate([before.astype(F32)[HALO - 8 :] * keep, block.astype(F32)], axis=0)
+
+    def conv(cols):
+        taps = taps_ref[:, cols]
+        before = edge_ref[:, cols].astype(F32)[HALO - 8 :] * taps[CONV_K : CONV_K + 1]
+        joined = jnp.concatenate([before, head_ref[:, cols].astype(F32)], axis=0)
         total = joined[5 : 5 + HALO] * taps[0:1]
         for k in range(1, CONV_K):
             total = total + joined[5 + k : 5 + k + HALO] * taps[k : k + 1]
         return silu_half(total)
 
-    bc = conv(edge_ref[:, b_cols], head_ref[:, b_cols], wbc_ref[0])
+    bc = conv(b_cols)
     bt = jnp.concatenate([bc, jnp.zeros((STATE - HALO, STATE), F32)], axis=0).T[:, 0:HALO].astype(BF16)
 
     for i in range(width // LANES):
         cols = slice(i * LANES, (i + 1) * LANES)
-        v = conv(edge_ref[:, cols], head_ref[:, cols], wx_ref[:, cols])
+        v = conv(cols)
         xs = (v * scale_ref[:, cols]).astype(BF16)
         state = end_ref[:, cols] + mm(bt, xs)
         both = jnp.concatenate([state, chain_ref[:, cols]], axis=0)
@@ -355,13 +355,13 @@
 
 
 def norm_kernel(
-    in_ref, a1_all, f1_all, cc_hbm, a0_hbm, f0_hbm, roll_hbm, gain_hbm, roll0_hbm, roll1_hbm, out_hbm, sums_ref,
-    entering, gated, a0_all, f0_all, roll_all, out_all, cc_ref, gain_ref, roll0_ref, roll1_ref, sums,
+    in_ref, a1_all, f1_all, cc_ref, a0_hbm, f0_hbm, roll_hbm, gain_hbm, roll0_hbm, roll1_hbm, out_hbm, sums_ref,
+    entering, gated, a0_all, f0_all, roll_all, out_all, gain_ref, roll0_ref, roll1_ref, sums,
     in_sems, out_sems, small_sems,
 ):
     width = out_all.shape[1]
     chunks, half = out_all.shape[0] // CHUNK, a0_all.shape[1]
-    pairs = [(cc_hbm, cc_ref), (a0_hbm, a0_all), (f0_hbm, f0_all), (roll_hbm, roll_all)]
+    pairs = [(a0_hbm, a0_all), (f0_hbm, f0_all), (roll_hbm, roll_all)]
     smalls = [(gain_hbm, gain_ref), (roll0_hbm, roll0_ref), (roll1_hbm, roll1_ref)]
     size = 2 * CHUNK
 
@@ -473,15 +473,16 @@
 
     vmem = pl.BlockSpec(memory_space=pltpu.VMEM)
     hbm = pl.BlockSpec(memory_space=pl.ANY)
-    end, head_scale, chain, head = pl.pallas_call(
+    end, head_scale, chain, head, taps = pl.pallas_call(
         functools.partial(state_kernel, chunks),
         in_specs=[smem, smem, hbm] + [vmem] * 5,
-        out_specs=[vmem] * 4,
+        out_specs=[vmem] * 5,
         out_shape=[
             jax.ShapeDtypeStruct((STATE, width), F32),
             jax.ShapeDtypeStruct((HALO, width), F32),
             jax.ShapeDtypeStruct((8, width), F32),
             jax.ShapeDtypeStruct((HALO, width + STATE), BF16),
+            jax.ShapeDtypeStruct((8, width + STATE), F32),
         ],
         scratch_shapes=[
             pltpu.VMEM((blocks, rows, LANES), BF16),
@@ -490,7 +491,7 @@
             pltpu.VMEM((rows, 256), BF16),
             pltpu.VMEM((blocks, rows, LANES), F32),
             pltpu.VMEM((STATE, rows), BF16),
-            pltpu.VMEM((rows, LANES), BF16),
+            pltpu.VMEM((blocks, rows, LANES), BF16),
             pltpu.SemaphoreType.DMA((blocks,)),
         ],
         compiler_params=grant(16),
@@ -498,19 +499,13 @@
         name="states",
     )(seq_spans, rank, x_values, b_values, steps_row, rate_row, conv_x, conv_bc)
 
-    msg, edge = pl.pallas_call(
-        functools.partial(edge_kernel, chunks),
-        grid=(1,),
-        in_specs=[
-            smem, smem, whole(HALO, ends), whole(HALO, width + STATE), whole(CONV_K, width),
-            whole(2, CONV_K, STATE), whole(HALO, width), whole(STATE, width), whole(8, width),
-        ],
-        out_specs=[whole(ring, 40, 128), whole(HALO, ends)],
-        out_shape=[jax.ShapeDtypeStruct((ring, 40, 128), BF16), pltpu.HBM((HALO, ends), BF16)],
+    msg = pl.pallas_call(
+        edge_kernel,
+        out_shape=pltpu.VMEM((ring, 40, 128), BF16),
         compiler_params=grant(8),
         name="edge_states",
-    )(seq_spans, rank, edge, head, conv_x, conv_bc, head_scale, end, chain)
-    (edge,) = in_hbm(edge)
+    )(edge, head, taps, head_scale, end, chain)
+    edge = pltpu.with_memory_space_constraint(edge, pltpu.VMEM)
 
     spread = lax.all_to_all(msg, "seq", split_axis=0, concat_axis=0, tiled=True)
 
@@ -557,10 +552,11 @@
         [
             pltpu.HBM((rows, 256), BF16),
             pltpu.HBM((chunks, STATE, CHUNK), BF16),
-            pltpu.HBM((rows, STATE), BF16),
+            pltpu.VMEM((rows, STATE), BF16),
         ],
     )
-    a0, f0, roll0, left, bt, cc = in_hbm(a0, f0, roll0, left, bt, cc)
+    a0, f0, roll0, left, bt = in_hbm(a0, f0, roll0, left, bt)
+    cc = pltpu.with_memory_space_constraint(cc, pltpu.VMEM)
     a1, f1, roll1 = mix(blocks // 2, shared_specs, [left, bt], [], [])
     a1, f1 = (pltpu.with_memory_space_constraint(v, pltpu.VMEM) for v in (a1, f1))
     (roll1,) = in_hbm(roll1)
@@ -568,7 +564,7 @@
     entering = pl.pallas_call(
         scan_kernel,
         in_specs=[pl.BlockSpec(memory_space=pltpu.VMEM), pl.BlockSpec(memory_space=pl.ANY)],
-        out_shape=jax.ShapeDtypeStruct((ring, 32, 128), BF16),
+        out_shape=pltpu.VMEM((ring, 32, 128), BF16),
         compiler_params=grant(8),
         name="scan",
     )(spread, roll0)
@@ -577,15 +573,15 @@
     group = lax.axis_size("head")
     normed, sums = pl.pallas_call(
         norm_kernel,
-        in_specs=[vmem] * 3 + [hbm] * 7,
+        in_specs=[vmem] * 4 + [hbm] * 6,
         out_specs=[hbm, vmem],
         out_shape=[pltpu.HBM((rows, width), BF16), jax.ShapeDtypeStruct((group, 2 * chunks, CHUNK), F32)],
         scratch_shapes=[pltpu.VMEM((STATE, width), BF16), pltpu.VMEM((2, CHUNK, width), F32)]
         + [pltpu.VMEM((rows, width // 2), BF16)] * 2
         + [pltpu.VMEM((rows, width), BF16)] * 2
-        + [pltpu.VMEM((rows, STATE), BF16), pltpu.VMEM((1, width), F32)]
+        + [pltpu.VMEM((1, width), F32)]
         + [pltpu.VMEM((chunks, CHUNK), F32)] * 3
-        + [pltpu.SemaphoreType.DMA((n, chunks // 2)) for n in (4,)]
+        + [pltpu.SemaphoreType.DMA((3, chunks // 2))]
         + [pltpu.SemaphoreType.DMA((chunks // 2,)), pltpu.SemaphoreType.DMA((3,))],
         compiler_params=grant(24),
         cost_estimate=pl.CostEstimate(flops=1 << 28, bytes_accessed=8 << 20, transcendentals=1 << 10),

time: 71.6 us -> 69.8 us (0.975)
  Pallas kernels: 30 us -> 27.8 us
    pallas_call x2, Pallas kernels: 7.46 us -> 6.6 us  [the longest x1 5.58 us: shards(): pl.pallas_call(norm_kernel, in_specs=[vmem] * 4 + [hbm] * 6, out_specs=[h...]
    pallas_call x1, Pallas kernels: 6.65 us -> 5.79 us  [shards(): pl.pallas_call(functools.partial(state_kernel, chunks), in_specs=[smem, s...]
  transfers between devices with their start and end apart: 3 -> 3, of which waited for: 2 -> 2; matrix products, arithmetic and copies ran while one was open for 0% -> 0% of each run, Pallas kernels for 29% -> 28%
where the time goes in v2:
time: 69.8 us; the launch traced here: 69.4 us
  Pallas kernels  27.8 us (40%)
  starting transfers between devices  21.6 us (31%)
  blocking collectives  12.9 us (18%)
  waiting for transfers between devices  5.81 us (8%)
    pallas_call x2, Pallas kernels, mix(): pl.pallas_call(functools.partial(mix_kernel, chunks, first * LANES), grid...  13.8 us
    all_to_all x1, blocking collectives, shards(): lax.all_to_all(sums, 'head', split_axis=0, concat_axis=0, tiled=True)  12.9 us
    all_to_all x1, starting transfers between devices, shards(): spread = lax.all_to_all(msg, 'seq', split_axis=0, concat_axis=0, tiled=True)  10.1 us
    all_to_all x1, starting transfers between devices, shards(): lax.all_to_all(entering, 'seq', split_axis=0, concat_axis=0, tiled=True)  7.1 us
    pallas_call x1, Pallas kernels, shards(): pl.pallas_call(functools.partial(state_kernel, chunks), in_specs=[smem, s...  5.79 us
    pallas_call x1, Pallas kernels, shards(): pl.pallas_call(norm_kernel, in_specs=[vmem] * 4 + [hbm] * 6, out_specs=[h...  5.58 us
    ppermute x1, starting transfers between devices, shards(): edge = lax.ppermute(edge, 'seq', [(i, i + 1) for i in range(ring - 1)])  4.36 us
    all_to_all x1, waiting for transfers between devices, shards(): lax.all_to_all(entering, 'seq', split_axis=0, concat_axis=0, tiled=True)  3.22 us
  transfers between devices with their start and end apart: 3, of which 2 were waited for; matrix products, arithmetic and copies ran while one was open for 0% of the time, Pallas kernels for 28%

profile of v2, /device:TPU:1, one launch (start us, length us, event | category | flops | bytes accessed | tf_op | source)
XLA Modules:
  0.0 69.4 jit_solution(15457834118019830314)
XLA Ops:
  0.6 0.8 %tails.1 = bf16[16,1280]{1,0:T(8,128)(2,1)S(1)} custom-call(bf16[1024,1024]{1,0:T(8,128)(2,1)} %x_ref.5, bf16[1024,128]{1,0:T(8,128)(2,1)} %refs_0_.1, bf16[1024,128]{1,0:T(8,128)(2,1)} %refs_1_.1), custom_call_target="tpu_custom_call" | custom-call | tf_op jit(solution)/shard_map/tails/pallas_call | solution.py:461
  1.4 4.4 %collective-permute-start = (bf16[16,1280]{1,0:T(8,128)(2,1)S(1)}, bf16[16,1280]{1,0:T(8,128)(2,1)S(1)}, u32[]{:S(2)}, u32[]{:S(2)}) collective-permute-start(bf16[16,1280]{1,0:T(8,128)(2,1)S(1)} %tails.1), channel_id=1, source_target_pairs={{0,8},{8,16},{16,24},{24,32},{32,40},{40,48},{48,56},{56,64},{64,7... | collective-permute-start | bytes 122888 | tf_op jit(solution)/shard_map/ppermute | solution.py:470
  5.8 5.8 %states.1 = (f32[128,1024]{1,0:T(8,128)S(1)}, f32[16,1024]{1,0:T(8,128)S(1)}, f32[8,1024]{1,0:T(8,128)S(1)}, bf16[16,1152]{1,0:T(8,128)(2,1)S(1)}, f32[8,1152]{1,0:T(8,128)S(1)}) custom-call(s32[4]{0:T(128)} %seq_ref.5, s32[1]{0:T(128)} %bitcast.rank_ref, bf16[1024,1024]{1,0:T(8,128)(2,1)} %x_ref.5, bf16[1024,128]{1,0:T(8,128)(2,1)} %refs_0_.1, ...), custom_call_target="tpu_custom_call" | custom-call | flops 536870912 | bytes 4194304 | tf_op jit(solution)/shard_map/states/pallas_call | solution.py:476
  11.6 0.0 collective-permute-done.edge_ref.refs_2_
  11.6 1.0 %edge_states.1 = bf16[32,40,128]{2,1,0:T(8,128)(2,1)} custom-call(bf16[16,1280]{1,0:T(8,128)(2,1)S(1)} %collective-permute-done.edge_ref.refs_2_, bf16[16,1152]{1,0:T(8,128)(2,1)S(1)} %get-tuple-element.18.head_ref, f32[8,1152]{1,0:T(8,128)S(1)} %get-tuple-element.19.taps_ref, f32[16,1024]{1,0:T(8,128)S(1)} %get-tuple-element.20.scale_ref, ...), custom_call_target="tpu_custom_call" | custom-call | tf_op jit(solution)/shard_map/edge_states/pallas_call | solution.py:502
  12.6 10.1 %all-to-all-start = ((bf16[32,40,128]{2,1,0:T(8,128)(2,1)}), bf16[32,40,128]{2,1,0:T(8,128)(2,1)S(1)}, u32[]{:S(2)}, u32[]{:S(2)}) async-start(bf16[32,40,128]{2,1,0:T(8,128)(2,1)} %edge_states.1), calls=%async_computation | async-start | bytes 655360 | tf_op jit(solution)/shard_map/all_to_all | solution.py:510
  22.8 7.4 %mix_first.1 = (bf16[1024,512]{1,0:T(8,128)(2,1)}, bf16[1024,512]{1,0:T(8,128)(2,1)}, f32[8,128]{1,0:T(8,128)}, bf16[1024,256]{1,0:T(8,128)(2,1)}, bf16[8,128,12...) custom-call(s32[4]{0:T(128)} %seq_ref.5, s32[1]{0:T(128)} %bitcast.rank_ref, bf16[1024,1024]{1,0:T(8,128)(2,1)} %x_ref.5, ...), custom_call_target="tpu_custom_call" | custom-call | flops 1073741824 | bytes 9437184 | tf_op jit(solution)/shard_map/mix_first/pallas_call | solution.py:515
  30.1 2.6 %all-to-all-done.in_ref = bf16[32,40,128]{2,1,0:T(8,128)(2,1)S(1)} async-done(((bf16[32,40,128]{2,1,0:T(8,128)(2,1)}), bf16[32,40,128]{2,1,0:T(8,128)(2,1)S(1)}, u32[]{:S(2)}, u32[]{:S(2)}) %all-to-all-start) | async-done | bytes 327712 | tf_op jit(solution)/shard_map/all_to_all | solution.py:510
  32.7 0.8 %scan.1 = bf16[32,32,128]{2,1,0:T(8,128)(2,1)} custom-call(bf16[32,40,128]{2,1,0:T(8,128)(2,1)S(1)} %all-to-all-done.in_ref, f32[8,128]{1,0:T(8,128)} %get-tuple-element.23.after_ref.roll0_hbm), custom_call_target="tpu_custom_call" | custom-call | tf_op jit(solution)/shard_map/scan/pallas_call | solution.py:564
  33.5 7.1 %all-to-all-start.1 = ((bf16[32,32,128]{2,1,0:T(8,128)(2,1)}), bf16[32,32,128]{2,1,0:T(8,128)(2,1)S(1)}, u32[]{:S(2)}, u32[]{:S(2)}) async-start(bf16[32,32,128]{2,1,0:T(8,128)(2,1)} %scan.1), calls=%async_computation.1 | async-start | bytes 524288 | tf_op jit(solution)/shard_map/all_to_all | solution.py:571
  40.6 6.5 %mix_second.1 = (bf16[1024,512]{1,0:T(8,128)(2,1)S(1)}, bf16[1024,512]{1,0:T(8,128)(2,1)S(1)}, f32[8,128]{1,0:T(8,128)}) custom-call(s32[4]{0:T(128)} %seq_ref.5, s32[1]{0:T(128)} %bitcast.rank_ref, bf16[1024,1024]{1,0:T(8,128)(2,1)} %x_ref.5, bf16[16,1280]{1,0:T(8,128)(2,1)S(1)} %collective-permute-done.edge_ref.refs_2_, f32[16,1024]{1,0:T(8,128)} %bitcast.9, ...), custom_call_target="tpu_custom_call" | custom-call | flops 1073741824 | bytes 9437184 | tf_op jit(solution)/shard_map/mix_second/pallas_call | solution.py:515
  47.1 3.2 %all-to-all-done.1.in_ref = bf16[32,32,128]{2,1,0:T(8,128)(2,1)S(1)} async-done(((bf16[32,32,128]{2,1,0:T(8,128)(2,1)}), bf16[32,32,128]{2,1,0:T(8,128)(2,1)S(1)}, u32[]{:S(2)}, u32[]{:S(2)}) %all-to-all-start.1) | async-done | bytes 262176 | tf_op jit(solution)/shard_map/all_to_all | solution.py:571
  50.3 5.6 %norms.1 = (bf16[1024,1024]{1,0:T(8,128)(2,1)}, f32[8,16,128]{2,1,0:T(8,128)S(1)}) custom-call(bf16[32,32,128]{2,1,0:T(8,128)(2,1)S(1)} %all-to-all-done.1.in_ref, bf16[1024,512]{1,0:T(8,128)(2,1)S(1)} %get-tuple-element.26.a1_all, bf16[1024,512]{1,0:T(8,128)(2,1)S(1)} %get-tuple-element.27.f1_all, bf16[1024,128]{1,0:T(8,128)(2,1)S(1)} %get-tuple-element.28.cc_ref, ...), custom_call_target="tpu_custom_call" | custom-call | flops 268435456 | bytes 8388608 | tf_op jit(solution)/shard_map/norms/pallas_call | solution.py:574
  55.9 12.9 %all_to_all.15 = f32[8,16,128]{2,1,0:T(8,128)S(1)} all-to-all(f32[8,16,128]{2,1,0:T(8,128)S(1)} %get-tuple-element.33), channel_id=1, replica_groups=mesh['seq'=32,'head'=8] {'head'}, dimensions={0} | all-to-all | bytes 131072 | tf_op jit(solution)/shard_map/all_to_all | solution.py:591
  68.8 0.6 fusion.2
  (1 shorter events, 0.0 us)
Async XLA Ops:
  1.4 10.2 %collective-permute-start = (bf16[16,1280]{1,0:T(8,128)(2,1)S(1)}, bf16[16,1280]{1,0:T(8,128)(2,1)S(1)}, u32[]{:S(2)}, u32[]{:S(2)}) collective-permute-start(bf16[16,1280]{1,0:T(8,128)(2,1)S(1)} %tails.1), channel_id=1, source_target_pairs={{0,8},{8,16},{16,24},{24,32},{32,40},{40,48},{48,56},{56,64},{64,7... | collective-permute-start | bytes 122888 | tf_op jit(solution)/shard_map/ppermute | solution.py:470
  12.6 20.1 %all-to-all-start = ((bf16[32,40,128]{2,1,0:T(8,128)(2,1)}), bf16[32,40,128]{2,1,0:T(8,128)(2,1)S(1)}, u32[]{:S(2)}, u32[]{:S(2)}) async-start(bf16[32,40,128]{2,1,0:T(8,128)(2,1)} %edge_states.1), calls=%async_computation | async-start | bytes 655360 | tf_op jit(solution)/shard_map/all_to_all | solution.py:510
  33.5 16.8 %all-to-all-start.1 = ((bf16[32,32,128]{2,1,0:T(8,128)(2,1)}), bf16[32,32,128]{2,1,0:T(8,128)(2,1)S(1)}, u32[]{:S(2)}, u32[]{:S(2)}) async-start(bf16[32,32,128]{2,1,0:T(8,128)(2,1)} %scan.1), calls=%async_computation.1 | async-start | bytes 524288 | tf_op jit(solution)/shard_map/all_to_all | solution.py:571

commit v3 on v2

--- a/solution.py
+++ b/solution.py
@@ -16,6 +16,7 @@
 CHUNK = 128
 LANES = 256
 HALO = 16
+MSG = 34
 
 F32 = jnp.float32
 BF16 = jnp.bfloat16
@@ -121,16 +122,31 @@
     padded_ref[8 : 8 + CHUNK, :] = src_ref[k * CHUNK : (k + 1) * CHUNK, lanes].astype(F32)
 
 
-def tail_kernel(x_ref, b_ref, c_ref, out_ref):
+def tail_kernel(
+    chunks, seq_ref, rank_ref, x_ref, b_ref, c_ref, b_all_ref, ts_ref, rate_ref, wx_ref, wbc_ref,
+    tail_ref, b_out, ts_out, rate_out, taps_ref, keep_ref,
+):
     width = x_ref.shape[1]
-    out_ref[:, 0:width] = x_ref[...]
-    out_ref[:, width : width + STATE] = b_ref[...]
-    out_ref[:, width + STATE : width + 2 * STATE] = c_ref[...]
+    tail_ref[:, 0:width] = x_ref[...]
+    tail_ref[:, width : width + STATE] = b_ref[...]
+    tail_ref[:, width + STATE : width + 2 * STATE] = c_ref[...]
+    b_out[...] = b_all_ref[...]
+    ts_out[...] = ts_ref[...]
+    rate_out[...] = rate_ref[...]
+    taps_ref[...] = jnp.zeros_like(taps_ref)
+    taps_ref[0:CONV_K, 0:width] = wx_ref[...].astype(F32) * 0.5
+    taps_ref[0:CONV_K, width : width + STATE] = wbc_ref[0].astype(F32) * 0.5
+    keeps = [v for v in chunk_keeps(chunks, seq_ref, rank_ref) if v is not None]
+    row = lax.broadcasted_iota(jnp.int32, (8, 128), 0)
+    flags = jnp.ones((8, 128), F32)
+    for i, keep in enumerate(keeps):
+        flags = jnp.where(row == i, keep, flags)
+    keep_ref[...] = flags
 
 
 def state_kernel(
-    chunks, seq_ref, rank_ref, x_hbm, b_ref, ts_ref, rate_ref, wx_ref, wb_ref,
-    end_ref, head_scale_ref, chain_ref, head_ref, taps_ref,
+    chunks, x_hbm, b_ref, ts_ref, rate_ref, taps_ref, keep_ref,
+    end_ref, head_scale_ref, chain_ref, head_ref,
     x_all, padded, order, lhsu, wide, bt, xs, x_sems,
 ):
     blocks = x_all.shape[0]
@@ -160,7 +176,7 @@
     reached = jnp.ones((16, 128), F32)
     whole = jnp.exp(later + totals)
     for n in range(0, chunks, SPAN // CHUNK):
-        keep = span_keep(seq_ref, rank_ref[0] * (chunks * CHUNK // SPAN) + n * CHUNK // SPAN)
+        keep = keep_ref[n * CHUNK // SPAN : n * CHUNK // SPAN + 1, :]
         reached = jnp.where(lane < n * heads, reached * keep, reached)
         whole = whole * keep
     scale = jnp.exp(after[0:CHUNK] + later[0:1]) * steps * reached[0:1]
@@ -173,13 +189,14 @@
         wide[i] = wide_all[:, i * LANES : (i + 1) * LANES]
     head_scale_ref[...] = mm(jnp.concatenate(split2(scale[0:HALO]), axis=1), e)
     row = lax.broadcasted_iota(jnp.int32, (16, 1), 0)
-    p1, p2, p3 = parts3(whole)
-    p = jnp.where(row == 0, p1.astype(F32), jnp.where(row == 1, p2.astype(F32), p3.astype(F32)))
-    chain_ref[...] = mm(jnp.where(row < 3, p, 0.0).astype(BF16), e[0:128])[0:8]
-    taps = wb_ref[0].astype(F32) * 0.5
+    hi, low = split2(whole)
+    p = jnp.where(row == 0, hi.astype(F32), jnp.where(row == 1, low.astype(F32), 0.0))
+    chain_ref[...] = mm(p.astype(BF16), e[0:128])[0:8]
+    taps = taps_ref[0:CONV_K, width : width + STATE]
     none = jnp.zeros((8, 128), F32)
 
-    keeps = chunk_keeps(chunks, seq_ref, rank_ref)
+    per_span = SPAN // CHUNK
+    keeps = [None if k % per_span else keep_ref[k // per_span : k // per_span + 1, :] for k in range(chunks)]
     for k in range(chunks):
         pad = padded.at[k % 4]
         fill_padded(pad, b_ref, none, k, slice(0, STATE), keeps[k])
@@ -188,15 +205,12 @@
             v = jnp.where((lax.broadcasted_iota(jnp.int32, v.shape, 0) & 7) == 0, 0.0, v)
         bt[:, k * CHUNK : (k + 1) * CHUNK] = v.T.astype(BF16)
     head_ref[:, width : width + STATE] = b_ref[0:HALO, :]
-    taps_ref[0:CONV_K, 0:width] = wx_ref[...].astype(F32) * 0.5
-    taps_ref[0:CONV_K, width : width + STATE] = taps
-    taps_ref[CONV_K : CONV_K + 1, :] = jnp.ones((1, width + STATE), F32) * keeps[0]
 
     def block(i, carry):
         lane0 = pl.multiple_of(i * LANES, LANES)
         lanes = pl.ds(lane0, LANES)
         x_ref = x_all.at[i]
-        weights = wx_ref[:, lanes].astype(F32) * 0.5
+        weights = taps_ref[0:CONV_K, lanes]
         x_copy(i).wait()
         head_ref[:, lanes] = x_ref[0:HALO, :]
 
@@ -215,13 +229,13 @@
         end_ref[:, i * LANES : (i + 1) * LANES] = mm(bt[...], xs[i])
 
 
-def edge_kernel(edge_ref, head_ref, taps_ref, scale_ref, end_ref, chain_ref, msg_ref):
+def edge_kernel(edge_ref, head_ref, taps_ref, keep_ref, scale_ref, end_ref, chain_ref, msg_ref, flat):
     width = end_ref.shape[1]
     b_cols = slice(width, width + STATE)
 
     def conv(cols):
         taps = taps_ref[:, cols]
-        before = edge_ref[:, cols].astype(F32)[HALO - 8 :] * taps[CONV_K : CONV_K + 1]
+        before = edge_ref[:, cols].astype(F32)[HALO - 8 :] * keep_ref[0:1, 0:1]
         joined = jnp.concatenate([before, head_ref[:, cols].astype(F32)], axis=0)
         total = joined[5 : 5 + HALO] * taps[0:1]
         for k in range(1, CONV_K):
@@ -236,25 +250,24 @@
         v = conv(cols)
         xs = (v * scale_ref[:, cols]).astype(BF16)
         state = end_ref[:, cols] + mm(bt, xs)
-        both = jnp.concatenate([state, chain_ref[:, cols]], axis=0)
+        decay = chain_ref[0 : MSG - 32, cols]
         for part in range(LANES // 128):
-            piece = both[:, part * 128 : (part + 1) * 128]
+            block = slice(part * 128, (part + 1) * 128)
             for nb in range(4):
-                own = jnp.concatenate([piece[nb * 32 : (nb + 1) * 32], piece[STATE:]], axis=0)
-                msg_ref[(i * (LANES // 128) + part) * 4 + nb] = own.astype(BF16)
-
-
-def scan_kernel(in_ref, after_ref, out_ref):
-    def some(m, carried):
-        for n in range(8):
-            i = 8 * m + n
-            out_ref[i] = carried.astype(BF16)
-            block = in_ref[i].astype(F32)
-            decay = block[32:33] + (block[33:34] + block[34:35])
-            carried = carried * decay + block[0:32]
-        return carried
-
-    lax.fori_loop(0, in_ref.shape[0] // 8, some, jnp.zeros((32, 128), F32))
+                first = MSG * ((i * (LANES // 128) + part) * 4 + nb)
+                flat[first : first + 32, :] = state[nb * 32 : (nb + 1) * 32, block]
+                flat[first + 32 : first + MSG, :] = decay[:, block]
+    msg_ref[...] = flat[...].astype(BF16)
+
+
+def scan_kernel(in_ref, after_ref, out_ref, flat):
+    flat[...] = in_ref[...].astype(F32)
+    carried = jnp.zeros((32, 128), F32)
+    for i in range(out_ref.shape[0]):
+        first = MSG * i
+        out_ref[i] = carried.astype(BF16)
+        decay = flat[first + 32 : first + 33, :] + flat[first + 33 : first + 34, :]
+        carried = carried * decay + flat[first : first + 32, :]
 
 
 def mix_first(chunks, seq_ref, rank_ref, b_ref, c_ref, edge_ref, wbc_ref, left, bt, cc_ref, padded):
@@ -385,18 +398,16 @@
     for lb in range(width // 128):
         for nb in range(4):
             entering[nb * 32 : (nb + 1) * 32, lb * 128 : (lb + 1) * 128] = in_ref[lb * 4 + nb]
-    for i in range(len(smalls)):
-        copy_small(i).wait()
-
     def two(m, carry):
-        for i in range(len(pairs)):
-            copy_in(i, m).wait()
         scales = []
         for n in range(2):
             toks = pl.ds(pl.multiple_of(m * size + n * CHUNK, CHUNK), CHUNK)
             squares = jnp.zeros((CHUNK, 128), F32)
-            for lane in range(0, width, LANES):
+            for lane in [*range(half, width, LANES), *range(0, half, LANES)]:
                 cols = slice(lane, lane + LANES)
+                if n == 0 and lane == 0:
+                    copy_in(0, m).wait()
+                    copy_in(1, m).wait()
                 a_ref, f_ref = (a0_all, f0_all) if lane < half else (a1_all, f1_all)
                 own = slice(lane % half, lane % half + LANES)
                 g = a_ref[toks, own].astype(F32) + f_ref[toks, own].astype(F32) * mm(cc_ref[toks, :], entering[:, cols])
@@ -405,8 +416,15 @@
                 squares = squares + (g[:, 0:128] + g[:, 128:256])
             mean = jnp.sum(squares, axis=1, keepdims=True) * (1.0 / width)
             scales.append(lax.rsqrt(mean + 1e-05))
+        copy_in(2, m).wait()
+
+        @pl.when(m == 0)
+        def _():
+            copy_small(0).wait()
+
         for n in range(2):
-            toks = pl.ds(pl.multiple_of(m * size + n * CHUNK, CHUNK), CHUNK)
+            k = 2 * m + n
+            toks = pl.ds(pl.multiple_of(k * CHUNK, CHUNK), CHUNK)
             squares = jnp.zeros((CHUNK, 128), F32)
             for lane in range(0, width, 128):
                 cols = slice(lane, lane + 128)
@@ -414,11 +432,13 @@
                 out_all[toks, cols] = v
                 d = v.astype(F32) - roll_all[toks, cols].astype(F32)
                 squares = squares + d * d
-            sums[pl.ds(2 * m + n, 1), :] = jnp.sum(squares.T, axis=0, keepdims=True)
+            sums[pl.ds(k, 1), :] = jnp.sum(squares.T, axis=0, keepdims=True)
         copy_out(m).start()
         return carry
 
     lax.fori_loop(0, chunks // 2, two, 0)
+    copy_small(1).wait()
+    copy_small(2).wait()
     both = jnp.concatenate([sums[...], roll0_ref[...] + roll1_ref[...]], axis=0)
     for i in range(sums_ref.shape[0]):
         sums_ref[i] = both
@@ -458,31 +478,41 @@
         time_steps.T, decay_rate.reshape(1, heads), skip_gain.reshape(1, heads), norm_gain.reshape(1, width), conv_x, conv_bc
     )
     last = rows // HALO - 1
-    edge = pl.pallas_call(
-        tail_kernel,
+    vmem = pl.BlockSpec(memory_space=pltpu.VMEM)
+    hbm = pl.BlockSpec(memory_space=pl.ANY)
+    edge, b_near, steps_near, rate_near, taps, keeps = pl.pallas_call(
+        functools.partial(tail_kernel, chunks),
         grid=(1,),
-        in_specs=[pl.BlockSpec((HALO, n), lambda i: (last, 0)) for n in (width, STATE, STATE)],
-        out_specs=whole(HALO, ends),
-        out_shape=jax.ShapeDtypeStruct((HALO, ends), BF16),
+        in_specs=[smem, smem]
+        + [pl.BlockSpec((HALO, n), lambda i: (last, 0)) for n in (width, STATE, STATE)]
+        + [whole(rows, STATE), whole(heads, rows), whole(1, heads), whole(CONV_K, width), whole(2, CONV_K, STATE)],
+        out_specs=[
+            whole(HALO, ends), whole(rows, STATE), whole(heads, rows), whole(1, heads), whole(8, width + STATE), whole(8, 128),
+        ],
+        out_shape=[
+            jax.ShapeDtypeStruct((HALO, ends), BF16),
+            pltpu.VMEM((rows, STATE), BF16),
+            pltpu.VMEM((heads, rows), F32),
+            pltpu.VMEM((1, heads), F32),
+            pltpu.VMEM((8, width + STATE), F32),
+            pltpu.VMEM((8, 128), F32),
+        ],
         compiler_params=grant(8),
         name="tails",
-    )(x_values, b_values, c_values)
+    )(seq_spans, rank, x_values, b_values, c_values, b_values, steps_row, rate_row, conv_x, conv_bc)
     edge = lax.ppermute(edge, "seq", [(i, i + 1) for i in range(ring - 1)])
     conv_scratch = pltpu.VMEM((4, 8 + CHUNK, 128), F32)
     wide_scratch = pltpu.VMEM((rows, LANES), F32)
 
-    vmem = pl.BlockSpec(memory_space=pltpu.VMEM)
-    hbm = pl.BlockSpec(memory_space=pl.ANY)
-    end, head_scale, chain, head, taps = pl.pallas_call(
+    end, head_scale, chain, head = pl.pallas_call(
         functools.partial(state_kernel, chunks),
-        in_specs=[smem, smem, hbm] + [vmem] * 5,
-        out_specs=[vmem] * 5,
+        in_specs=[hbm] + [vmem] * 5,
+        out_specs=[vmem] * 4,
         out_shape=[
             jax.ShapeDtypeStruct((STATE, width), F32),
             jax.ShapeDtypeStruct((HALO, width), F32),
             jax.ShapeDtypeStruct((8, width), F32),
             jax.ShapeDtypeStruct((HALO, width + STATE), BF16),
-            jax.ShapeDtypeStruct((8, width + STATE), F32),
         ],
         scratch_shapes=[
             pltpu.VMEM((blocks, rows, LANES), BF16),
@@ -497,17 +527,19 @@
         compiler_params=grant(16),
         cost_estimate=pl.CostEstimate(flops=1 << 29, bytes_accessed=4 << 20, transcendentals=1 << 20),
         name="states",
-    )(seq_spans, rank, x_values, b_values, steps_row, rate_row, conv_x, conv_bc)
+    )(x_values, b_near, steps_near, rate_near, taps, keeps)
 
     msg = pl.pallas_call(
         edge_kernel,
-        out_shape=pltpu.VMEM((ring, 40, 128), BF16),
+        out_shape=jax.ShapeDtypeStruct((ring * MSG, 128), BF16),
+        scratch_shapes=[pltpu.VMEM((ring * MSG, 128), F32)],
         compiler_params=grant(8),
         name="edge_states",
-    )(edge, head, taps, head_scale, end, chain)
+    )(edge, head, taps, keeps, head_scale, end, chain)
     edge = pltpu.with_memory_space_constraint(edge, pltpu.VMEM)
 
-    spread = lax.all_to_all(msg, "seq", split_axis=0, concat_axis=0, tiled=True)
+    msg = msg.reshape(ring, MSG // 2, 2, 128)
+    spread = lax.all_to_all(msg, "seq", split_axis=0, concat_axis=0, tiled=True).reshape(ring * MSG, 128)
 
     def mix(first, specs, operands, more_specs, more_shapes):
         half = blocks // 2
@@ -564,7 +596,8 @@
     entering = pl.pallas_call(
         scan_kernel,
         in_specs=[pl.BlockSpec(memory_space=pltpu.VMEM), pl.BlockSpec(memory_space=pl.ANY)],
-        out_shape=pltpu.VMEM((ring, 32, 128), BF16),
+        out_shape=jax.ShapeDtypeStruct((ring, 32, 128), BF16),
+        scratch_shapes=[pltpu.VMEM((ring * MSG, 128), F32)],
         compiler_params=grant(8),
         name="scan",
     )(spread, roll0)

time: 69.8 us -> 68.8 us (0.986)
    pallas_call x3, Pallas kernels: 7.6 us -> 6.9 us  [the longest x1 4.76 us: shards(): pl.pallas_call(functools.partial(state_kernel, chunks), in_specs=[hbm] +...]
  transfers between devices with their start and end apart: 3 -> 3, of which waited for: 2 -> 2; matrix products, arithmetic and copies ran while one was open for 0% -> 0% of each run, Pallas kernels for 28% -> 27%
where the time goes in v3:
time: 68.8 us; the launch traced here: 68.4 us
  Pallas kernels  27.5 us (40%)
  starting transfers between devices  21.4 us (31%)
  blocking collectives  12.7 us (18%)
  waiting for transfers between devices  5.57 us (8%)
  between operations  0.7 us (1%)
    pallas_call x2, Pallas kernels, mix(): pl.pallas_call(functools.partial(mix_kernel, chunks, first * LANES), grid...  13.8 us
    all_to_all x1, blocking collectives, shards(): lax.all_to_all(sums, 'head', split_axis=0, concat_axis=0, tiled=True)  12.7 us
    all_to_all x1, starting transfers between devices, shards(): lax.all_to_all(msg, 'seq', split_axis=0, concat_axis=0, tiled=True)  10.1 us
    all_to_all x1, starting transfers between devices, shards(): lax.all_to_all(entering, 'seq', split_axis=0, concat_axis=0, tiled=True)  6.87 us
    pallas_call x1, Pallas kernels, shards(): pl.pallas_call(norm_kernel, in_specs=[vmem] * 4 + [hbm] * 6, out_specs=[h...  5.96 us
    pallas_call x1, Pallas kernels, shards(): pl.pallas_call(functools.partial(state_kernel, chunks), in_specs=[hbm] +...  4.76 us
    ppermute x1, starting transfers between devices, shards(): edge = lax.ppermute(edge, 'seq', [(i, i + 1) for i in range(ring - 1)])  4.37 us
    all_to_all x1, waiting for transfers between devices, shards(): lax.all_to_all(entering, 'seq', split_axis=0, concat_axis=0, tiled=True)  3.2 us
  transfers between devices with their start and end apart: 3, of which 2 were waited for; matrix products, arithmetic and copies ran while one was open for 0% of the time, Pallas kernels for 27%

profile of v3, /device:TPU:1, one launch (start us, length us, event | category | flops | bytes accessed | tf_op | source)
XLA Modules:
  0.0 68.4 jit_solution(7052568199697199235)
XLA Ops:
  0.6 1.1 %tails.1 = (bf16[16,1280]{1,0:T(8,128)(2,1)S(1)}, bf16[1024,128]{1,0:T(8,128)(2,1)S(1)}, f32[16,1024]{1,0:T(8,128)S(1)}, f32[1,16]{1,0:T(1,128)S(1)}, f32[8,1152]{1,0:T(8,128)S(1)}, /*index=5*/f32[8,128]{1,0:T(8,128)S(1)}) custom-call(s32[4]{0:T(128)} %seq_ref.5, s32[1]{0:T(128)} %bitcast.rank_ref, bf16[1024,1024]{1,0:T(8,128)(2,1)} %x_ref.5, ...), custom_call_target="tpu_custom_call" | custom-call | tf_op jit(solution)/shard_map/tails/pallas_call | solution.py:483
  1.7 4.4 %collective-permute-start = (bf16[16,1280]{1,0:T(8,128)(2,1)S(1)}, bf16[16,1280]{1,0:T(8,128)(2,1)S(1)}, u32[]{:S(2)}, u32[]{:S(2)}) collective-permute-start(bf16[16,1280]{1,0:T(8,128)(2,1)S(1)} %get-tuple-element.23), channel_id=1, source_target_pairs={{0,8},{8,16},{16,24},{24,32},{32,40},{40,48},{48,56},{56,64},{64,7... | collective-permute-start | bytes 122888 | tf_op jit(solution)/shard_map/ppermute | solution.py:503
  6.1 4.8 %states.1 = (f32[128,1024]{1,0:T(8,128)S(1)}, f32[16,1024]{1,0:T(8,128)S(1)}, f32[8,1024]{1,0:T(8,128)S(1)}, bf16[16,1152]{1,0:T(8,128)(2,1)S(1)}) custom-call(bf16[1024,1024]{1,0:T(8,128)(2,1)} %x_ref.5, bf16[1024,128]{1,0:T(8,128)(2,1)S(1)} %get-tuple-element.24.b_ref, f32[16,1024]{1,0:T(8,128)S(1)} %get-tuple-element.25.ts_ref, ...), custom_call_target="tpu_custom_call" | custom-call | flops 536870912 | bytes 4194304 | tf_op jit(solution)/shard_map/states/pallas_call | solution.py:507
  10.9 0.0 collective-permute-done.edge_ref.refs_2_
  10.9 1.1 %edge_states.1 = bf16[1088,128]{1,0:T(8,128)(2,1)} custom-call(bf16[16,1280]{1,0:T(8,128)(2,1)S(1)} %collective-permute-done.edge_ref.refs_2_, bf16[16,1152]{1,0:T(8,128)(2,1)S(1)} %get-tuple-element.29.head_ref, f32[8,1152]{1,0:T(8,128)S(1)} %get-tuple-element.27.taps_ref, f32[8,128]{1,0:T(8,128)S(1)} %get-tuple-element.28.keep_ref, ...), custom_call_target="tpu_custom_call" | custom-call | tf_op jit(solution)/shard_map/edge_states/pallas_call | solution.py:532
  11.9 10.1 %all-to-all-start = ((bf16[32,17,2,128]{3,2,1,0:T(2,128)(2,1)}), bf16[32,17,2,128]{3,2,1,0:T(2,128)(2,1)S(1)}, u32[]{:S(2)}, u32[]{:S(2)}) async-start(bf16[32,17,2,128]{3,2,1,0:T(2,128)(2,1)} %bitcast.3), calls=%async_computation | async-start | bytes 557056 | tf_op jit(solution)/shard_map/all_to_all | solution.py:542
  22.1 7.4 %mix_first.1 = (bf16[1024,512]{1,0:T(8,128)(2,1)}, bf16[1024,512]{1,0:T(8,128)(2,1)}, f32[8,128]{1,0:T(8,128)}, bf16[1024,256]{1,0:T(8,128)(2,1)}, bf16[8,128,12...) custom-call(s32[4]{0:T(128)} %seq_ref.5, s32[1]{0:T(128)} %bitcast.rank_ref, bf16[1024,1024]{1,0:T(8,128)(2,1)} %x_ref.5, ...), custom_call_target="tpu_custom_call" | custom-call | flops 1073741824 | bytes 9437184 | tf_op jit(solution)/shard_map/mix_first/pallas_call | solution.py:547
  29.4 2.4 %all-to-all-done = bf16[32,17,2,128]{3,2,1,0:T(2,128)(2,1)S(1)} async-done(((bf16[32,17,2,128]{3,2,1,0:T(2,128)(2,1)}), bf16[32,17,2,128]{3,2,1,0:T(2,128)(2,1)S(1)}, u32[]{:S(2)}, u32[]{:S(2)}) %all-to-all-start) | async-done | bytes 278560 | tf_op jit(solution)/shard_map/all_to_all | solution.py:542
  31.8 0.8 %scan.1 = bf16[32,32,128]{2,1,0:T(8,128)(2,1)} custom-call(bf16[1088,128]{1,0:T(8,128)(2,1)S(1)} %bitcast.9, f32[8,128]{1,0:T(8,128)} %get-tuple-element.33.after_ref.roll0_hbm), custom_call_target="tpu_custom_call" | custom-call | tf_op jit(solution)/shard_map/scan/pallas_call | solution.py:596
  32.6 6.9 %all-to-all-start.1 = ((bf16[32,32,128]{2,1,0:T(8,128)(2,1)}), bf16[32,32,128]{2,1,0:T(8,128)(2,1)S(1)}, u32[]{:S(2)}, u32[]{:S(2)}) async-start(bf16[32,32,128]{2,1,0:T(8,128)(2,1)} %scan.1), calls=%async_computation.1 | async-start | bytes 524288 | tf_op jit(solution)/shard_map/all_to_all | solution.py:604
  39.5 6.5 %mix_second.1 = (bf16[1024,512]{1,0:T(8,128)(2,1)S(1)}, bf16[1024,512]{1,0:T(8,128)(2,1)S(1)}, f32[8,128]{1,0:T(8,128)}) custom-call(s32[4]{0:T(128)} %seq_ref.5, s32[1]{0:T(128)} %bitcast.rank_ref, bf16[1024,1024]{1,0:T(8,128)(2,1)} %x_ref.5, bf16[16,1280]{1,0:T(8,128)(2,1)S(1)} %collective-permute-done.edge_ref.refs_2_, f32[16,1024]{1,0:T(8,128)} %bitcast.12, ...), custom_call_target="tpu_custom_call" | custom-call | flops 1073741824 | bytes 9437184 | tf_op jit(solution)/shard_map/mix_second/pallas_call | solution.py:547
  45.9 3.2 %all-to-all-done.1.in_ref = bf16[32,32,128]{2,1,0:T(8,128)(2,1)S(1)} async-done(((bf16[32,32,128]{2,1,0:T(8,128)(2,1)}), bf16[32,32,128]{2,1,0:T(8,128)(2,1)S(1)}, u32[]{:S(2)}, u32[]{:S(2)}) %all-to-all-start.1) | async-done | bytes 262176 | tf_op jit(solution)/shard_map/all_to_all | solution.py:604
  49.1 6.0 %norms.1 = (bf16[1024,1024]{1,0:T(8,128)(2,1)}, f32[8,16,128]{2,1,0:T(8,128)S(1)}) custom-call(bf16[32,32,128]{2,1,0:T(8,128)(2,1)S(1)} %all-to-all-done.1.in_ref, bf16[1024,512]{1,0:T(8,128)(2,1)S(1)} %get-tuple-element.36.a1_all, bf16[1024,512]{1,0:T(8,128)(2,1)S(1)} %get-tuple-element.37.f1_all, bf16[1024,128]{1,0:T(8,128)(2,1)S(1)} %get-tuple-element.38.cc_ref, ...), custom_call_target="tpu_custom_call" | custom-call | flops 268435456 | bytes 8388608 | tf_op jit(solution)/shard_map/norms/pallas_call | solution.py:607
  55.1 12.7 %all_to_all.15 = f32[8,16,128]{2,1,0:T(8,128)S(1)} all-to-all(f32[8,16,128]{2,1,0:T(8,128)S(1)} %get-tuple-element.43), channel_id=1, replica_groups=mesh['seq'=32,'head'=8] {'head'}, dimensions={0} | all-to-all | bytes 131072 | tf_op jit(solution)/shard_map/all_to_all | solution.py:624
  67.8 0.6 fusion.2
  (1 shorter events, 0.0 us)
Async XLA Ops:
  1.7 9.2 %collective-permute-start = (bf16[16,1280]{1,0:T(8,128)(2,1)S(1)}, bf16[16,1280]{1,0:T(8,128)(2,1)S(1)}, u32[]{:S(2)}, u32[]{:S(2)}) collective-permute-start(bf16[16,1280]{1,0:T(8,128)(2,1)S(1)} %get-tuple-element.23), channel_id=1, source_target_pairs={{0,8},{8,16},{16,24},{24,32},{32,40},{40,48},{48,56},{56,64},{64,7... | collective-permute-start | bytes 122888 | tf_op jit(solution)/shard_map/ppermute | solution.py:503
  11.9 19.9 %all-to-all-start = ((bf16[32,17,2,128]{3,2,1,0:T(2,128)(2,1)}), bf16[32,17,2,128]{3,2,1,0:T(2,128)(2,1)S(1)}, u32[]{:S(2)}, u32[]{:S(2)}) async-start(bf16[32,17,2,128]{3,2,1,0:T(2,128)(2,1)} %bitcast.3), calls=%async_computation | async-start | bytes 557056 | tf_op jit(solution)/shard_map/all_to_all | solution.py:542
  32.6 16.5 %all-to-all-start.1 = ((bf16[32,32,128]{2,1,0:T(8,128)(2,1)}), bf16[32,32,128]{2,1,0:T(8,128)(2,1)S(1)}, u32[]{:S(2)}, u32[]{:S(2)}) async-start(bf16[32,32,128]{2,1,0:T(8,128)(2,1)} %scan.1), calls=%async_computation.1 | async-start | bytes 524288 | tf_op jit(solution)/shard_map/all_to_all | solution.py:604

commit v4 on v3

--- a/solution.py
+++ b/solution.py
@@ -398,30 +398,26 @@
     for lb in range(width // 128):
         for nb in range(4):
             entering[nb * 32 : (nb + 1) * 32, lb * 128 : (lb + 1) * 128] = in_ref[lb * 4 + nb]
+    for i in range(len(smalls)):
+        copy_small(i).wait()
+
     def two(m, carry):
+        for i in range(len(pairs)):
+            copy_in(i, m).wait()
         scales = []
         for n in range(2):
             toks = pl.ds(pl.multiple_of(m * size + n * CHUNK, CHUNK), CHUNK)
             squares = jnp.zeros((CHUNK, 128), F32)
-            for lane in [*range(half, width, LANES), *range(0, half, LANES)]:
-                cols = slice(lane, lane + LANES)
-                if n == 0 and lane == 0:
-                    copy_in(0, m).wait()
-                    copy_in(1, m).wait()
+            for lane in range(0, width, LANES):
                 a_ref, f_ref = (a0_all, f0_all) if lane < half else (a1_all, f1_all)
-                own = slice(lane % half, lane % half + LANES)
-                g = a_ref[toks, own].astype(F32) + f_ref[toks, own].astype(F32) * mm(cc_ref[toks, :], entering[:, cols])
-                gated[n, :, cols] = g
-                g = g * g
-                squares = squares + (g[:, 0:128] + g[:, 128:256])
+                q = mm(cc_ref[toks, :], entering[:, lane : lane + LANES])
+                for part in range(0, LANES, 128):
+                    own = slice(lane % half + part, lane % half + part + 128)
+                    g = a_ref[toks, own].astype(F32) + f_ref[toks, own].astype(F32) * q[:, part : part + 128]
+                    gated[n, :, lane + part : lane + part + 128] = g
+                    squares = squares + g * g
             mean = jnp.sum(squares, axis=1, keepdims=True) * (1.0 / width)
             scales.append(lax.rsqrt(mean + 1e-05))
-        copy_in(2, m).wait()
-
-        @pl.when(m == 0)
-        def _():
-            copy_small(0).wait()
-
         for n in range(2):
             k = 2 * m + n
             toks = pl.ds(pl.multiple_of(k * CHUNK, CHUNK), CHUNK)
@@ -437,8 +433,6 @@
         return carry
 
     lax.fori_loop(0, chunks // 2, two, 0)
-    copy_small(1).wait()
-    copy_small(2).wait()
     both = jnp.concatenate([sums[...], roll0_ref[...] + roll1_ref[...]], axis=0)
     for i in range(sums_ref.shape[0]):
         sums_ref[i] = both

time: 68.8 us -> 68.4 us (level)
  no operation moved by 1% of the time
where the time goes in v4:
time: 68.4 us; the launch traced here: 68.1 us
  Pallas kernels  27.1 us (40%)
  starting transfers between devices  21.4 us (31%)
  blocking collectives  12.7 us (19%)
  waiting for transfers between devices  5.57 us (8%)
  between operations  0.7 us (1%)
    pallas_call x2, Pallas kernels, mix(): pl.pallas_call(functools.partial(mix_kernel, chunks, first * LANES), grid...  13.8 us
    all_to_all x1, blocking collectives, shards(): lax.all_to_all(sums, 'head', split_axis=0, concat_axis=0, tiled=True)  12.7 us
    all_to_all x1, starting transfers between devices, shards(): lax.all_to_all(msg, 'seq', split_axis=0, concat_axis=0, tiled=True)  10.1 us
    all_to_all x1, starting transfers between devices, shards(): lax.all_to_all(entering, 'seq', split_axis=0, concat_axis=0, tiled=True)  6.87 us
    pallas_call x1, Pallas kernels, shards(): pl.pallas_call(norm_kernel, in_specs=[vmem] * 4 + [hbm] * 6, out_specs=[h...  5.57 us
    pallas_call x1, Pallas kernels, shards(): pl.pallas_call(functools.partial(state_kernel, chunks), in_specs=[hbm] +...  4.76 us
    ppermute x1, starting transfers between devices, shards(): edge = lax.ppermute(edge, 'seq', [(i, i + 1) for i in range(ring - 1)])  4.37 us
    all_to_all x1, waiting for transfers between devices, shards(): lax.all_to_all(entering, 'seq', split_axis=0, concat_axis=0, tiled=True)  3.2 us
  transfers between devices with their start and end apart: 3, of which 2 were waited for; matrix products, arithmetic and copies ran while one was open for 0% of the time, Pallas kernels for 27%

profile of v4, /device:TPU:1, one launch (start us, length us, event | category | flops | bytes accessed | tf_op | source)
XLA Modules:
  0.0 68.1 jit_solution(8557839108109112227)
XLA Ops:
  0.6 1.1 %tails.1 = (bf16[16,1280]{1,0:T(8,128)(2,1)S(1)}, bf16[1024,128]{1,0:T(8,128)(2,1)S(1)}, f32[16,1024]{1,0:T(8,128)S(1)}, f32[1,16]{1,0:T(1,128)S(1)}, f32[8,1152]{1,0:T(8,128)S(1)}, /*index=5*/f32[8,128]{1,0:T(8,128)S(1)}) custom-call(s32[4]{0:T(128)} %seq_ref.5, s32[1]{0:T(128)} %bitcast.rank_ref, bf16[1024,1024]{1,0:T(8,128)(2,1)} %x_ref.5, ...), custom_call_target="tpu_custom_call" | custom-call | tf_op jit(solution)/shard_map/tails/pallas_call | solution.py:477
  1.7 4.4 %collective-permute-start = (bf16[16,1280]{1,0:T(8,128)(2,1)S(1)}, bf16[16,1280]{1,0:T(8,128)(2,1)S(1)}, u32[]{:S(2)}, u32[]{:S(2)}) collective-permute-start(bf16[16,1280]{1,0:T(8,128)(2,1)S(1)} %get-tuple-element.23), channel_id=1, source_target_pairs={{0,8},{8,16},{16,24},{24,32},{32,40},{40,48},{48,56},{56,64},{64,7... | collective-permute-start | bytes 122888 | tf_op jit(solution)/shard_map/ppermute | solution.py:497
  6.1 4.8 %states.1 = (f32[128,1024]{1,0:T(8,128)S(1)}, f32[16,1024]{1,0:T(8,128)S(1)}, f32[8,1024]{1,0:T(8,128)S(1)}, bf16[16,1152]{1,0:T(8,128)(2,1)S(1)}) custom-call(bf16[1024,1024]{1,0:T(8,128)(2,1)} %x_ref.5, bf16[1024,128]{1,0:T(8,128)(2,1)S(1)} %get-tuple-element.24.b_ref, f32[16,1024]{1,0:T(8,128)S(1)} %get-tuple-element.25.ts_ref, ...), custom_call_target="tpu_custom_call" | custom-call | flops 536870912 | bytes 4194304 | tf_op jit(solution)/shard_map/states/pallas_call | solution.py:501
  10.9 0.0 collective-permute-done.edge_ref.refs_2_
  10.9 1.1 %edge_states.1 = bf16[1088,128]{1,0:T(8,128)(2,1)} custom-call(bf16[16,1280]{1,0:T(8,128)(2,1)S(1)} %collective-permute-done.edge_ref.refs_2_, bf16[16,1152]{1,0:T(8,128)(2,1)S(1)} %get-tuple-element.29.head_ref, f32[8,1152]{1,0:T(8,128)S(1)} %get-tuple-element.27.taps_ref, f32[8,128]{1,0:T(8,128)S(1)} %get-tuple-element.28.keep_ref, ...), custom_call_target="tpu_custom_call" | custom-call | tf_op jit(solution)/shard_map/edge_states/pallas_call | solution.py:526
  11.9 10.1 %all-to-all-start = ((bf16[32,17,2,128]{3,2,1,0:T(2,128)(2,1)}), bf16[32,17,2,128]{3,2,1,0:T(2,128)(2,1)S(1)}, u32[]{:S(2)}, u32[]{:S(2)}) async-start(bf16[32,17,2,128]{3,2,1,0:T(2,128)(2,1)} %bitcast.3), calls=%async_computation | async-start | bytes 557056 | tf_op jit(solution)/shard_map/all_to_all | solution.py:536
  22.1 7.4 %mix_first.1 = (bf16[1024,512]{1,0:T(8,128)(2,1)}, bf16[1024,512]{1,0:T(8,128)(2,1)}, f32[8,128]{1,0:T(8,128)}, bf16[1024,256]{1,0:T(8,128)(2,1)}, bf16[8,128,12...) custom-call(s32[4]{0:T(128)} %seq_ref.5, s32[1]{0:T(128)} %bitcast.rank_ref, bf16[1024,1024]{1,0:T(8,128)(2,1)} %x_ref.5, ...), custom_call_target="tpu_custom_call" | custom-call | flops 1073741824 | bytes 9437184 | tf_op jit(solution)/shard_map/mix_first/pallas_call | solution.py:541
  29.4 2.4 %all-to-all-done = bf16[32,17,2,128]{3,2,1,0:T(2,128)(2,1)S(1)} async-done(((bf16[32,17,2,128]{3,2,1,0:T(2,128)(2,1)}), bf16[32,17,2,128]{3,2,1,0:T(2,128)(2,1)S(1)}, u32[]{:S(2)}, u32[]{:S(2)}) %all-to-all-start) | async-done | bytes 278560 | tf_op jit(solution)/shard_map/all_to_all | solution.py:536
  31.8 0.8 %scan.1 = bf16[32,32,128]{2,1,0:T(8,128)(2,1)} custom-call(bf16[1088,128]{1,0:T(8,128)(2,1)S(1)} %bitcast.9, f32[8,128]{1,0:T(8,128)} %get-tuple-element.33.after_ref.roll0_hbm), custom_call_target="tpu_custom_call" | custom-call | tf_op jit(solution)/shard_map/scan/pallas_call | solution.py:590
  32.6 6.9 %all-to-all-start.1 = ((bf16[32,32,128]{2,1,0:T(8,128)(2,1)}), bf16[32,32,128]{2,1,0:T(8,128)(2,1)S(1)}, u32[]{:S(2)}, u32[]{:S(2)}) async-start(bf16[32,32,128]{2,1,0:T(8,128)(2,1)} %scan.1), calls=%async_computation.1 | async-start | bytes 524288 | tf_op jit(solution)/shard_map/all_to_all | solution.py:598
  39.5 6.5 %mix_second.1 = (bf16[1024,512]{1,0:T(8,128)(2,1)S(1)}, bf16[1024,512]{1,0:T(8,128)(2,1)S(1)}, f32[8,128]{1,0:T(8,128)}) custom-call(s32[4]{0:T(128)} %seq_ref.5, s32[1]{0:T(128)} %bitcast.rank_ref, bf16[1024,1024]{1,0:T(8,128)(2,1)} %x_ref.5, bf16[16,1280]{1,0:T(8,128)(2,1)S(1)} %collective-permute-done.edge_ref.refs_2_, f32[16,1024]{1,0:T(8,128)} %bitcast.12, ...), custom_call_target="tpu_custom_call" | custom-call | flops 1073741824 | bytes 9437184 | tf_op jit(solution)/shard_map/mix_second/pallas_call | solution.py:541
  45.9 3.2 %all-to-all-done.1.in_ref = bf16[32,32,128]{2,1,0:T(8,128)(2,1)S(1)} async-done(((bf16[32,32,128]{2,1,0:T(8,128)(2,1)}), bf16[32,32,128]{2,1,0:T(8,128)(2,1)S(1)}, u32[]{:S(2)}, u32[]{:S(2)}) %all-to-all-start.1) | async-done | bytes 262176 | tf_op jit(solution)/shard_map/all_to_all | solution.py:598
  49.1 5.6 %norms.1 = (bf16[1024,1024]{1,0:T(8,128)(2,1)}, f32[8,16,128]{2,1,0:T(8,128)S(1)}) custom-call(bf16[32,32,128]{2,1,0:T(8,128)(2,1)S(1)} %all-to-all-done.1.in_ref, bf16[1024,512]{1,0:T(8,128)(2,1)S(1)} %get-tuple-element.36.a1_all, bf16[1024,512]{1,0:T(8,128)(2,1)S(1)} %get-tuple-element.37.f1_all, bf16[1024,128]{1,0:T(8,128)(2,1)S(1)} %get-tuple-element.38.cc_ref, ...), custom_call_target="tpu_custom_call" | custom-call | flops 268435456 | bytes 8388608 | tf_op jit(solution)/shard_map/norms/pallas_call | solution.py:601
  54.7 12.7 %all_to_all.15 = f32[8,16,128]{2,1,0:T(8,128)S(1)} all-to-all(f32[8,16,128]{2,1,0:T(8,128)S(1)} %get-tuple-element.43), channel_id=1, replica_groups=mesh['seq'=32,'head'=8] {'head'}, dimensions={0} | all-to-all | bytes 131072 | tf_op jit(solution)/shard_map/all_to_all | solution.py:618
  67.4 0.6 fusion.2
  (1 shorter events, 0.0 us)
Async XLA Ops:
  1.7 9.2 %collective-permute-start = (bf16[16,1280]{1,0:T(8,128)(2,1)S(1)}, bf16[16,1280]{1,0:T(8,128)(2,1)S(1)}, u32[]{:S(2)}, u32[]{:S(2)}) collective-permute-start(bf16[16,1280]{1,0:T(8,128)(2,1)S(1)} %get-tuple-element.23), channel_id=1, source_target_pairs={{0,8},{8,16},{16,24},{24,32},{32,40},{40,48},{48,56},{56,64},{64,7... | collective-permute-start | bytes 122888 | tf_op jit(solution)/shard_map/ppermute | solution.py:497
  11.9 19.9 %all-to-all-start = ((bf16[32,17,2,128]{3,2,1,0:T(2,128)(2,1)}), bf16[32,17,2,128]{3,2,1,0:T(2,128)(2,1)S(1)}, u32[]{:S(2)}, u32[]{:S(2)}) async-start(bf16[32,17,2,128]{3,2,1,0:T(2,128)(2,1)} %bitcast.3), calls=%async_computation | async-start | bytes 557056 | tf_op jit(solution)/shard_map/all_to_all | solution.py:536
  32.6 16.5 %all-to-all-start.1 = ((bf16[32,32,128]{2,1,0:T(8,128)(2,1)}), bf16[32,32,128]{2,1,0:T(8,128)(2,1)S(1)}, u32[]{:S(2)}, u32[]{:S(2)}) async-start(bf16[32,32,128]{2,1,0:T(8,128)(2,1)} %scan.1), calls=%async_computation.1 | async-start | bytes 524288 | tf_op jit(solution)/shard_map/all_to_all | solution.py:598

commit v5 on v4

--- a/solution.py
+++ b/solution.py
@@ -369,7 +369,7 @@
 
 def norm_kernel(
     in_ref, a1_all, f1_all, cc_ref, a0_hbm, f0_hbm, roll_hbm, gain_hbm, roll0_hbm, roll1_hbm, out_hbm, sums_ref,
-    entering, gated, a0_all, f0_all, roll_all, out_all, gain_ref, roll0_ref, roll1_ref, sums,
+    gated, a0_all, f0_all, roll_all, out_all, gain_ref, roll0_ref, roll1_ref, parts,
     in_sems, out_sems, small_sems,
 ):
     width = out_all.shape[1]
@@ -395,9 +395,6 @@
         if m == 0:
             for i in range(len(smalls)):
                 copy_small(i).start()
-    for lb in range(width // 128):
-        for nb in range(4):
-            entering[nb * 32 : (nb + 1) * 32, lb * 128 : (lb + 1) * 128] = in_ref[lb * 4 + nb]
     for i in range(len(smalls)):
         copy_small(i).wait()
 
@@ -410,7 +407,8 @@
             squares = jnp.zeros((CHUNK, 128), F32)
             for lane in range(0, width, LANES):
                 a_ref, f_ref = (a0_all, f0_all) if lane < half else (a1_all, f1_all)
-                q = mm(cc_ref[toks, :], entering[:, lane : lane + LANES])
+                own = [in_ref[lb * 4 : lb * 4 + 4].reshape(STATE, 128) for lb in range(lane // 128, (lane + LANES) // 128)]
+                q = mm(cc_ref[toks, :], jnp.concatenate(own, axis=1))
                 for part in range(0, LANES, 128):
                     own = slice(lane % half + part, lane % half + part + 128)
                     g = a_ref[toks, own].astype(F32) + f_ref[toks, own].astype(F32) * q[:, part : part + 128]
@@ -428,12 +426,13 @@
                 out_all[toks, cols] = v
                 d = v.astype(F32) - roll_all[toks, cols].astype(F32)
                 squares = squares + d * d
-            sums[pl.ds(k, 1), :] = jnp.sum(squares.T, axis=0, keepdims=True)
+            parts[k] = squares
         copy_out(m).start()
         return carry
 
     lax.fori_loop(0, chunks // 2, two, 0)
-    both = jnp.concatenate([sums[...], roll0_ref[...] + roll1_ref[...]], axis=0)
+    sums = [jnp.sum(parts[k].T, axis=0, keepdims=True) for k in range(chunks)]
+    both = jnp.concatenate(sums + [roll0_ref[...] + roll1_ref[...]], axis=0)
     for i in range(sums_ref.shape[0]):
         sums_ref[i] = both
     for m in range(chunks // 2):
@@ -603,11 +602,12 @@
         in_specs=[vmem] * 4 + [hbm] * 6,
         out_specs=[hbm, vmem],
         out_shape=[pltpu.HBM((rows, width), BF16), jax.ShapeDtypeStruct((group, 2 * chunks, CHUNK), F32)],
-        scratch_shapes=[pltpu.VMEM((STATE, width), BF16), pltpu.VMEM((2, CHUNK, width), F32)]
+        scratch_shapes=[pltpu.VMEM((2, CHUNK, width), F32)]
         + [pltpu.VMEM((rows, width // 2), BF16)] * 2
         + [pltpu.VMEM((rows, width), BF16)] * 2
         + [pltpu.VMEM((1, width), F32)]
-        + [pltpu.VMEM((chunks, CHUNK), F32)] * 3
+        + [pltpu.VMEM((chunks, CHUNK), F32)] * 2
+        + [pltpu.VMEM((chunks, CHUNK, 128), F32)]
         + [pltpu.SemaphoreType.DMA((3, chunks // 2))]
         + [pltpu.SemaphoreType.DMA((chunks // 2,)), pltpu.SemaphoreType.DMA((3,))],
         compiler_params=grant(24),

time: 68.4 us -> 68.2 us (level)
  no operation moved by 1% of the time
where the time goes in v5:
time: 68.2 us; the launch traced here: 67.9 us
  Pallas kernels  26.9 us (39%)
  starting transfers between devices  21.4 us (31%)
  blocking collectives  12.7 us (19%)
  waiting for transfers between devices  5.57 us (8%)
  between operations  0.7 us (1%)
    pallas_call x2, Pallas kernels, mix(): pl.pallas_call(functools.partial(mix_kernel, chunks, first * LANES), grid...  13.8 us
    all_to_all x1, blocking collectives, shards(): lax.all_to_all(sums, 'head', split_axis=0, concat_axis=0, tiled=True)  12.7 us
    all_to_all x1, starting transfers between devices, shards(): lax.all_to_all(msg, 'seq', split_axis=0, concat_axis=0, tiled=True)  10.1 us
    all_to_all x1, starting transfers between devices, shards(): lax.all_to_all(entering, 'seq', split_axis=0, concat_axis=0, tiled=True)  6.87 us
    pallas_call x1, Pallas kernels, shards(): pl.pallas_call(norm_kernel, in_specs=[vmem] * 4 + [hbm] * 6, out_specs=[h...  5.38 us
    pallas_call x1, Pallas kernels, shards(): pl.pallas_call(functools.partial(state_kernel, chunks), in_specs=[hbm] +...  4.76 us
    ppermute x1, starting transfers between devices, shards(): edge = lax.ppermute(edge, 'seq', [(i, i + 1) for i in range(ring - 1)])  4.37 us
    all_to_all x1, waiting for transfers between devices, shards(): lax.all_to_all(entering, 'seq', split_axis=0, concat_axis=0, tiled=True)  3.2 us
  transfers between devices with their start and end apart: 3, of which 2 were waited for; matrix products, arithmetic and copies ran while one was open for 0% of the time, Pallas kernels for 27%

profile of v5, /device:TPU:1, one launch (start us, length us, event | category | flops | bytes accessed | tf_op | source)
XLA Modules:
  0.0 67.9 jit_solution(11436742239757317441)
XLA Ops:
  0.6 1.1 %tails.1 = (bf16[16,1280]{1,0:T(8,128)(2,1)S(1)}, bf16[1024,128]{1,0:T(8,128)(2,1)S(1)}, f32[16,1024]{1,0:T(8,128)S(1)}, f32[1,16]{1,0:T(1,128)S(1)}, f32[8,1152]{1,0:T(8,128)S(1)}, /*index=5*/f32[8,128]{1,0:T(8,128)S(1)}) custom-call(s32[4]{0:T(128)} %seq_ref.5, s32[1]{0:T(128)} %bitcast.rank_ref, bf16[1024,1024]{1,0:T(8,128)(2,1)} %x_ref.5, ...), custom_call_target="tpu_custom_call" | custom-call | tf_op jit(solution)/shard_map/tails/pallas_call | solution.py:476
  1.7 4.4 %collective-permute-start = (bf16[16,1280]{1,0:T(8,128)(2,1)S(1)}, bf16[16,1280]{1,0:T(8,128)(2,1)S(1)}, u32[]{:S(2)}, u32[]{:S(2)}) collective-permute-start(bf16[16,1280]{1,0:T(8,128)(2,1)S(1)} %get-tuple-element.23), channel_id=1, source_target_pairs={{0,8},{8,16},{16,24},{24,32},{32,40},{40,48},{48,56},{56,64},{64,7... | collective-permute-start | bytes 122888 | tf_op jit(solution)/shard_map/ppermute | solution.py:496
  6.1 4.8 %states.1 = (f32[128,1024]{1,0:T(8,128)S(1)}, f32[16,1024]{1,0:T(8,128)S(1)}, f32[8,1024]{1,0:T(8,128)S(1)}, bf16[16,1152]{1,0:T(8,128)(2,1)S(1)}) custom-call(bf16[1024,1024]{1,0:T(8,128)(2,1)} %x_ref.5, bf16[1024,128]{1,0:T(8,128)(2,1)S(1)} %get-tuple-element.24.b_ref, f32[16,1024]{1,0:T(8,128)S(1)} %get-tuple-element.25.ts_ref, ...), custom_call_target="tpu_custom_call" | custom-call | flops 536870912 | bytes 4194304 | tf_op jit(solution)/shard_map/states/pallas_call | solution.py:500
  10.9 0.0 collective-permute-done.edge_ref.refs_2_
  10.9 1.1 %edge_states.1 = bf16[1088,128]{1,0:T(8,128)(2,1)} custom-call(bf16[16,1280]{1,0:T(8,128)(2,1)S(1)} %collective-permute-done.edge_ref.refs_2_, bf16[16,1152]{1,0:T(8,128)(2,1)S(1)} %get-tuple-element.29.head_ref, f32[8,1152]{1,0:T(8,128)S(1)} %get-tuple-element.27.taps_ref, f32[8,128]{1,0:T(8,128)S(1)} %get-tuple-element.28.keep_ref, ...), custom_call_target="tpu_custom_call" | custom-call | tf_op jit(solution)/shard_map/edge_states/pallas_call | solution.py:525
  11.9 10.1 %all-to-all-start = ((bf16[32,17,2,128]{3,2,1,0:T(2,128)(2,1)}), bf16[32,17,2,128]{3,2,1,0:T(2,128)(2,1)S(1)}, u32[]{:S(2)}, u32[]{:S(2)}) async-start(bf16[32,17,2,128]{3,2,1,0:T(2,128)(2,1)} %bitcast.3), calls=%async_computation | async-start | bytes 557056 | tf_op jit(solution)/shard_map/all_to_all | solution.py:535
  22.1 7.4 %mix_first.1 = (bf16[1024,512]{1,0:T(8,128)(2,1)}, bf16[1024,512]{1,0:T(8,128)(2,1)}, f32[8,128]{1,0:T(8,128)}, bf16[1024,256]{1,0:T(8,128)(2,1)}, bf16[8,128,12...) custom-call(s32[4]{0:T(128)} %seq_ref.5, s32[1]{0:T(128)} %bitcast.rank_ref, bf16[1024,1024]{1,0:T(8,128)(2,1)} %x_ref.5, ...), custom_call_target="tpu_custom_call" | custom-call | flops 1073741824 | bytes 9437184 | tf_op jit(solution)/shard_map/mix_first/pallas_call | solution.py:540
  29.4 2.4 %all-to-all-done = bf16[32,17,2,128]{3,2,1,0:T(2,128)(2,1)S(1)} async-done(((bf16[32,17,2,128]{3,2,1,0:T(2,128)(2,1)}), bf16[32,17,2,128]{3,2,1,0:T(2,128)(2,1)S(1)}, u32[]{:S(2)}, u32[]{:S(2)}) %all-to-all-start) | async-done | bytes 278560 | tf_op jit(solution)/shard_map/all_to_all | solution.py:535
  31.8 0.8 %scan.1 = bf16[32,32,128]{2,1,0:T(8,128)(2,1)} custom-call(bf16[1088,128]{1,0:T(8,128)(2,1)S(1)} %bitcast.9, f32[8,128]{1,0:T(8,128)} %get-tuple-element.33.after_ref.roll0_hbm), custom_call_target="tpu_custom_call" | custom-call | tf_op jit(solution)/shard_map/scan/pallas_call | solution.py:589
  32.6 6.9 %all-to-all-start.1 = ((bf16[32,32,128]{2,1,0:T(8,128)(2,1)}), bf16[32,32,128]{2,1,0:T(8,128)(2,1)S(1)}, u32[]{:S(2)}, u32[]{:S(2)}) async-start(bf16[32,32,128]{2,1,0:T(8,128)(2,1)} %scan.1), calls=%async_computation.1 | async-start | bytes 524288 | tf_op jit(solution)/shard_map/all_to_all | solution.py:597
  39.5 6.5 %mix_second.1 = (bf16[1024,512]{1,0:T(8,128)(2,1)S(1)}, bf16[1024,512]{1,0:T(8,128)(2,1)S(1)}, f32[8,128]{1,0:T(8,128)}) custom-call(s32[4]{0:T(128)} %seq_ref.5, s32[1]{0:T(128)} %bitcast.rank_ref, bf16[1024,1024]{1,0:T(8,128)(2,1)} %x_ref.5, bf16[16,1280]{1,0:T(8,128)(2,1)S(1)} %collective-permute-done.edge_ref.refs_2_, f32[16,1024]{1,0:T(8,128)} %bitcast.12, ...), custom_call_target="tpu_custom_call" | custom-call | flops 1073741824 | bytes 9437184 | tf_op jit(solution)/shard_map/mix_second/pallas_call | solution.py:540
  45.9 3.2 %all-to-all-done.1.in_ref = bf16[32,32,128]{2,1,0:T(8,128)(2,1)S(1)} async-done(((bf16[32,32,128]{2,1,0:T(8,128)(2,1)}), bf16[32,32,128]{2,1,0:T(8,128)(2,1)S(1)}, u32[]{:S(2)}, u32[]{:S(2)}) %all-to-all-start.1) | async-done | bytes 262176 | tf_op jit(solution)/shard_map/all_to_all | solution.py:597
  49.1 5.4 %norms.1 = (bf16[1024,1024]{1,0:T(8,128)(2,1)}, f32[8,16,128]{2,1,0:T(8,128)S(1)}) custom-call(bf16[32,32,128]{2,1,0:T(8,128)(2,1)S(1)} %all-to-all-done.1.in_ref, bf16[1024,512]{1,0:T(8,128)(2,1)S(1)} %get-tuple-element.36.a1_all, bf16[1024,512]{1,0:T(8,128)(2,1)S(1)} %get-tuple-element.37.f1_all, bf16[1024,128]{1,0:T(8,128)(2,1)S(1)} %get-tuple-element.38.cc_ref, ...), custom_call_target="tpu_custom_call" | custom-call | flops 268435456 | bytes 8388608 | tf_op jit(solution)/shard_map/norms/pallas_call | solution.py:600
  54.5 12.7 %all_to_all.15 = f32[8,16,128]{2,1,0:T(8,128)S(1)} all-to-all(f32[8,16,128]{2,1,0:T(8,128)S(1)} %get-tuple-element.43), channel_id=1, replica_groups=mesh['seq'=32,'head'=8] {'head'}, dimensions={0} | all-to-all | bytes 131072 | tf_op jit(solution)/shard_map/all_to_all | solution.py:618
  67.2 0.6 fusion.2
  (1 shorter events, 0.0 us)
Async XLA Ops:
  1.7 9.2 %collective-permute-start = (bf16[16,1280]{1,0:T(8,128)(2,1)S(1)}, bf16[16,1280]{1,0:T(8,128)(2,1)S(1)}, u32[]{:S(2)}, u32[]{:S(2)}) collective-permute-start(bf16[16,1280]{1,0:T(8,128)(2,1)S(1)} %get-tuple-element.23), channel_id=1, source_target_pairs={{0,8},{8,16},{16,24},{24,32},{32,40},{40,48},{48,56},{56,64},{64,7... | collective-permute-start | bytes 122888 | tf_op jit(solution)/shard_map/ppermute | solution.py:496
  11.9 19.9 %all-to-all-start = ((bf16[32,17,2,128]{3,2,1,0:T(2,128)(2,1)}), bf16[32,17,2,128]{3,2,1,0:T(2,128)(2,1)S(1)}, u32[]{:S(2)}, u32[]{:S(2)}) async-start(bf16[32,17,2,128]{3,2,1,0:T(2,128)(2,1)} %bitcast.3), calls=%async_computation | async-start | bytes 557056 | tf_op jit(solution)/shard_map/all_to_all | solution.py:535
  32.6 16.5 %all-to-all-start.1 = ((bf16[32,32,128]{2,1,0:T(8,128)(2,1)}), bf16[32,32,128]{2,1,0:T(8,128)(2,1)S(1)}, u32[]{:S(2)}, u32[]{:S(2)}) async-start(bf16[32,32,128]{2,1,0:T(8,128)(2,1)} %scan.1), calls=%async_computation.1 | async-start | bytes 524288 | tf_op jit(solution)/shard_map/all_to_all | solution.py:597

commit v6 on v5

--- a/solution.py
+++ b/solution.py
@@ -369,7 +369,7 @@
 
 def norm_kernel(
     in_ref, a1_all, f1_all, cc_ref, a0_hbm, f0_hbm, roll_hbm, gain_hbm, roll0_hbm, roll1_hbm, out_hbm, sums_ref,
-    gated, a0_all, f0_all, roll_all, out_all, gain_ref, roll0_ref, roll1_ref, parts,
+    gated, gated_near, a0_all, f0_all, roll_all, out_all, gain_ref, roll0_ref, roll1_ref, parts,
     in_sems, out_sems, small_sems,
 ):
     width = out_all.shape[1]
@@ -395,6 +395,31 @@
         if m == 0:
             for i in range(len(smalls)):
                 copy_small(i).start()
+    def gate(k, lanes, a_ref, f_ref, put, squares):
+        toks = pl.ds(pl.multiple_of(k * CHUNK, CHUNK), CHUNK)
+        first = lanes[0]
+        for lane in lanes:
+            own = [in_ref[lb * 4 : lb * 4 + 4].reshape(STATE, 128) for lb in range(lane // 128, (lane + LANES) // 128)]
+            q = mm(cc_ref[toks, :], jnp.concatenate(own, axis=1))
+            for part in range(0, LANES, 128):
+                cols = slice(lane - first + part, lane - first + part + 128)
+                g = a_ref[toks, cols].astype(F32) + f_ref[toks, cols].astype(F32) * q[:, part : part + 128]
+                put(cols, g)
+                squares = squares + g * g
+        return squares
+
+    def near(m, carry):
+        for n in range(2):
+            k = 2 * m + n
+            toks = pl.ds(pl.multiple_of(k * CHUNK, CHUNK), CHUNK)
+
+            def put(cols, g):
+                gated_near[toks, cols] = g
+
+            parts[k] = gate(k, range(half, width, LANES), a1_all, f1_all, put, jnp.zeros((CHUNK, 128), F32))
+        return carry
+
+    lax.fori_loop(0, chunks // 2, near, 0)
     for i in range(len(smalls)):
         copy_small(i).wait()
 
@@ -403,17 +428,11 @@
             copy_in(i, m).wait()
         scales = []
         for n in range(2):
-            toks = pl.ds(pl.multiple_of(m * size + n * CHUNK, CHUNK), CHUNK)
-            squares = jnp.zeros((CHUNK, 128), F32)
-            for lane in range(0, width, LANES):
-                a_ref, f_ref = (a0_all, f0_all) if lane < half else (a1_all, f1_all)
-                own = [in_ref[lb * 4 : lb * 4 + 4].reshape(STATE, 128) for lb in range(lane // 128, (lane + LANES) // 128)]
-                q = mm(cc_ref[toks, :], jnp.concatenate(own, axis=1))
-                for part in range(0, LANES, 128):
-                    own = slice(lane % half + part, lane % half + part + 128)
-                    g = a_ref[toks, own].astype(F32) + f_ref[toks, own].astype(F32) * q[:, part : part + 128]
-                    gated[n, :, lane + part : lane + part + 128] = g
-                    squares = squares + g * g
+
+            def put(cols, g):
+                gated[n, :, cols] = g
+
+            squares = gate(2 * m + n, range(0, half, LANES), a0_all, f0_all, put, parts[2 * m + n])
             mean = jnp.sum(squares, axis=1, keepdims=True) * (1.0 / width)
             scales.append(lax.rsqrt(mean + 1e-05))
         for n in range(2):
@@ -422,7 +441,8 @@
             squares = jnp.zeros((CHUNK, 128), F32)
             for lane in range(0, width, 128):
                 cols = slice(lane, lane + 128)
-                v = (gated[n, :, cols] * scales[n] * gain_ref[:, cols]).astype(BF16)
+                g = gated[n, :, cols] if lane < half else gated_near[toks, lane - half : lane - half + 128]
+                v = (g * scales[n] * gain_ref[:, cols]).astype(BF16)
                 out_all[toks, cols] = v
                 d = v.astype(F32) - roll_all[toks, cols].astype(F32)
                 squares = squares + d * d
@@ -602,7 +622,7 @@
         in_specs=[vmem] * 4 + [hbm] * 6,
         out_specs=[hbm, vmem],
         out_shape=[pltpu.HBM((rows, width), BF16), jax.ShapeDtypeStruct((group, 2 * chunks, CHUNK), F32)],
-        scratch_shapes=[pltpu.VMEM((2, CHUNK, width), F32)]
+        scratch_shapes=[pltpu.VMEM((2, CHUNK, width // 2), F32), pltpu.VMEM((rows, width // 2), F32)]
         + [pltpu.VMEM((rows, width // 2), BF16)] * 2
         + [pltpu.VMEM((rows, width), BF16)] * 2
         + [pltpu.VMEM((1, width), F32)]

time: 68.2 us -> 67.8 us (level)
  transfers between devices with their start and end apart: 3 -> 3, of which waited for: 2 -> 2; matrix products, arithmetic and copies ran while one was open for 0% -> 0% of each run, Pallas kernels for 27% -> 28%
where the time goes in v6:
time: 67.8 us; the launch traced here: 67.5 us
  Pallas kernels  26.5 us (39%)
  starting transfers between devices  21.4 us (32%)
  blocking collectives  12.7 us (19%)
  waiting for transfers between devices  5.57 us (8%)
  between operations  0.7 us (1%)
    pallas_call x2, Pallas kernels, mix(): pl.pallas_call(functools.partial(mix_kernel, chunks, first * LANES), grid...  13.8 us
    all_to_all x1, blocking collectives, shards(): lax.all_to_all(sums, 'head', split_axis=0, concat_axis=0, tiled=True)  12.7 us
    all_to_all x1, starting transfers between devices, shards(): lax.all_to_all(msg, 'seq', split_axis=0, concat_axis=0, tiled=True)  10.1 us
    all_to_all x1, starting transfers between devices, shards(): lax.all_to_all(entering, 'seq', split_axis=0, concat_axis=0, tiled=True)  6.87 us
    pallas_call x1, Pallas kernels, shards(): pl.pallas_call(norm_kernel, in_specs=[vmem] * 4 + [hbm] * 6, out_specs=[h...  4.97 us
    pallas_call x1, Pallas kernels, shards(): pl.pallas_call(functools.partial(state_kernel, chunks), in_specs=[hbm] +...  4.76 us
    ppermute x1, starting transfers between devices, shards(): edge = lax.ppermute(edge, 'seq', [(i, i + 1) for i in range(ring - 1)])  4.37 us
    all_to_all x1, waiting for transfers between devices, shards(): lax.all_to_all(entering, 'seq', split_axis=0, concat_axis=0, tiled=True)  3.2 us
  transfers between devices with their start and end apart: 3, of which 2 were waited for; matrix products, arithmetic and copies ran while one was open for 0% of the time, Pallas kernels for 28%

profile of v6, /device:TPU:1, one launch (start us, length us, event | category | flops | bytes accessed | tf_op | source)
XLA Modules:
  0.0 67.5 jit_solution(13870978968190764370)
XLA Ops:
  0.6 1.1 %tails.1 = (bf16[16,1280]{1,0:T(8,128)(2,1)S(1)}, bf16[1024,128]{1,0:T(8,128)(2,1)S(1)}, f32[16,1024]{1,0:T(8,128)S(1)}, f32[1,16]{1,0:T(1,128)S(1)}, f32[8,1152]{1,0:T(8,128)S(1)}, /*index=5*/f32[8,128]{1,0:T(8,128)S(1)}) custom-call(s32[4]{0:T(128)} %seq_ref.5, s32[1]{0:T(128)} %bitcast.rank_ref, bf16[1024,1024]{1,0:T(8,128)(2,1)} %x_ref.5, ...), custom_call_target="tpu_custom_call" | custom-call | tf_op jit(solution)/shard_map/tails/pallas_call | solution.py:496
  1.7 4.4 %collective-permute-start = (bf16[16,1280]{1,0:T(8,128)(2,1)S(1)}, bf16[16,1280]{1,0:T(8,128)(2,1)S(1)}, u32[]{:S(2)}, u32[]{:S(2)}) collective-permute-start(bf16[16,1280]{1,0:T(8,128)(2,1)S(1)} %get-tuple-element.23), channel_id=1, source_target_pairs={{0,8},{8,16},{16,24},{24,32},{32,40},{40,48},{48,56},{56,64},{64,7... | collective-permute-start | bytes 122888 | tf_op jit(solution)/shard_map/ppermute | solution.py:516
  6.1 4.8 %states.1 = (f32[128,1024]{1,0:T(8,128)S(1)}, f32[16,1024]{1,0:T(8,128)S(1)}, f32[8,1024]{1,0:T(8,128)S(1)}, bf16[16,1152]{1,0:T(8,128)(2,1)S(1)}) custom-call(bf16[1024,1024]{1,0:T(8,128)(2,1)} %x_ref.5, bf16[1024,128]{1,0:T(8,128)(2,1)S(1)} %get-tuple-element.24.b_ref, f32[16,1024]{1,0:T(8,128)S(1)} %get-tuple-element.25.ts_ref, ...), custom_call_target="tpu_custom_call" | custom-call | flops 536870912 | bytes 4194304 | tf_op jit(solution)/shard_map/states/pallas_call | solution.py:520
  10.9 0.0 collective-permute-done.edge_ref.refs_2_
  10.9 1.1 %edge_states.1 = bf16[1088,128]{1,0:T(8,128)(2,1)} custom-call(bf16[16,1280]{1,0:T(8,128)(2,1)S(1)} %collective-permute-done.edge_ref.refs_2_, bf16[16,1152]{1,0:T(8,128)(2,1)S(1)} %get-tuple-element.29.head_ref, f32[8,1152]{1,0:T(8,128)S(1)} %get-tuple-element.27.taps_ref, f32[8,128]{1,0:T(8,128)S(1)} %get-tuple-element.28.keep_ref, ...), custom_call_target="tpu_custom_call" | custom-call | tf_op jit(solution)/shard_map/edge_states/pallas_call | solution.py:545
  11.9 10.1 %all-to-all-start = ((bf16[32,17,2,128]{3,2,1,0:T(2,128)(2,1)}), bf16[32,17,2,128]{3,2,1,0:T(2,128)(2,1)S(1)}, u32[]{:S(2)}, u32[]{:S(2)}) async-start(bf16[32,17,2,128]{3,2,1,0:T(2,128)(2,1)} %bitcast.3), calls=%async_computation | async-start | bytes 557056 | tf_op jit(solution)/shard_map/all_to_all | solution.py:555
  22.1 7.4 %mix_first.1 = (bf16[1024,512]{1,0:T(8,128)(2,1)}, bf16[1024,512]{1,0:T(8,128)(2,1)}, f32[8,128]{1,0:T(8,128)}, bf16[1024,256]{1,0:T(8,128)(2,1)}, bf16[8,128,12...) custom-call(s32[4]{0:T(128)} %seq_ref.5, s32[1]{0:T(128)} %bitcast.rank_ref, bf16[1024,1024]{1,0:T(8,128)(2,1)} %x_ref.5, ...), custom_call_target="tpu_custom_call" | custom-call | flops 1073741824 | bytes 9437184 | tf_op jit(solution)/shard_map/mix_first/pallas_call | solution.py:560
  29.4 2.4 %all-to-all-done = bf16[32,17,2,128]{3,2,1,0:T(2,128)(2,1)S(1)} async-done(((bf16[32,17,2,128]{3,2,1,0:T(2,128)(2,1)}), bf16[32,17,2,128]{3,2,1,0:T(2,128)(2,1)S(1)}, u32[]{:S(2)}, u32[]{:S(2)}) %all-to-all-start) | async-done | bytes 278560 | tf_op jit(solution)/shard_map/all_to_all | solution.py:555
  31.8 0.8 %scan.1 = bf16[32,32,128]{2,1,0:T(8,128)(2,1)} custom-call(bf16[1088,128]{1,0:T(8,128)(2,1)S(1)} %bitcast.9, f32[8,128]{1,0:T(8,128)} %get-tuple-element.33.after_ref.roll0_hbm), custom_call_target="tpu_custom_call" | custom-call | tf_op jit(solution)/shard_map/scan/pallas_call | solution.py:609
  32.6 6.9 %all-to-all-start.1 = ((bf16[32,32,128]{2,1,0:T(8,128)(2,1)}), bf16[32,32,128]{2,1,0:T(8,128)(2,1)S(1)}, u32[]{:S(2)}, u32[]{:S(2)}) async-start(bf16[32,32,128]{2,1,0:T(8,128)(2,1)} %scan.1), calls=%async_computation.1 | async-start | bytes 524288 | tf_op jit(solution)/shard_map/all_to_all | solution.py:617
  39.5 6.5 %mix_second.1 = (bf16[1024,512]{1,0:T(8,128)(2,1)S(1)}, bf16[1024,512]{1,0:T(8,128)(2,1)S(1)}, f32[8,128]{1,0:T(8,128)}) custom-call(s32[4]{0:T(128)} %seq_ref.5, s32[1]{0:T(128)} %bitcast.rank_ref, bf16[1024,1024]{1,0:T(8,128)(2,1)} %x_ref.5, bf16[16,1280]{1,0:T(8,128)(2,1)S(1)} %collective-permute-done.edge_ref.refs_2_, f32[16,1024]{1,0:T(8,128)} %bitcast.12, ...), custom_call_target="tpu_custom_call" | custom-call | flops 1073741824 | bytes 9437184 | tf_op jit(solution)/shard_map/mix_second/pallas_call | solution.py:560
  45.9 3.2 %all-to-all-done.1.in_ref = bf16[32,32,128]{2,1,0:T(8,128)(2,1)S(1)} async-done(((bf16[32,32,128]{2,1,0:T(8,128)(2,1)}), bf16[32,32,128]{2,1,0:T(8,128)(2,1)S(1)}, u32[]{:S(2)}, u32[]{:S(2)}) %all-to-all-start.1) | async-done | bytes 262176 | tf_op jit(solution)/shard_map/all_to_all | solution.py:617
  49.1 5.0 %norms.1 = (bf16[1024,1024]{1,0:T(8,128)(2,1)}, f32[8,16,128]{2,1,0:T(8,128)S(1)}) custom-call(bf16[32,32,128]{2,1,0:T(8,128)(2,1)S(1)} %all-to-all-done.1.in_ref, bf16[1024,512]{1,0:T(8,128)(2,1)S(1)} %get-tuple-element.36.a1_all, bf16[1024,512]{1,0:T(8,128)(2,1)S(1)} %get-tuple-element.37.f1_all, bf16[1024,128]{1,0:T(8,128)(2,1)S(1)} %get-tuple-element.38.cc_ref, ...), custom_call_target="tpu_custom_call" | custom-call | flops 268435456 | bytes 8388608 | tf_op jit(solution)/shard_map/norms/pallas_call | solution.py:620
  54.1 12.7 %all_to_all.15 = f32[8,16,128]{2,1,0:T(8,128)S(1)} all-to-all(f32[8,16,128]{2,1,0:T(8,128)S(1)} %get-tuple-element.43), channel_id=1, replica_groups=mesh['seq'=32,'head'=8] {'head'}, dimensions={0} | all-to-all | bytes 131072 | tf_op jit(solution)/shard_map/all_to_all | solution.py:638
  66.8 0.6 fusion.2
  (1 shorter events, 0.0 us)
Async XLA Ops:
  1.7 9.2 %collective-permute-start = (bf16[16,1280]{1,0:T(8,128)(2,1)S(1)}, bf16[16,1280]{1,0:T(8,128)(2,1)S(1)}, u32[]{:S(2)}, u32[]{:S(2)}) collective-permute-start(bf16[16,1280]{1,0:T(8,128)(2,1)S(1)} %get-tuple-element.23), channel_id=1, source_target_pairs={{0,8},{8,16},{16,24},{24,32},{32,40},{40,48},{48,56},{56,64},{64,7... | collective-permute-start | bytes 122888 | tf_op jit(solution)/shard_map/ppermute | solution.py:516
  11.9 19.9 %all-to-all-start = ((bf16[32,17,2,128]{3,2,1,0:T(2,128)(2,1)}), bf16[32,17,2,128]{3,2,1,0:T(2,128)(2,1)S(1)}, u32[]{:S(2)}, u32[]{:S(2)}) async-start(bf16[32,17,2,128]{3,2,1,0:T(2,128)(2,1)} %bitcast.3), calls=%async_computation | async-start | bytes 557056 | tf_op jit(solution)/shard_map/all_to_all | solution.py:555
  32.6 16.5 %all-to-all-start.1 = ((bf16[32,32,128]{2,1,0:T(8,128)(2,1)}), bf16[32,32,128]{2,1,0:T(8,128)(2,1)S(1)}, u32[]{:S(2)}, u32[]{:S(2)}) async-start(bf16[32,32,128]{2,1,0:T(8,128)(2,1)} %scan.1), calls=%async_computation.1 | async-start | bytes 524288 | tf_op jit(solution)/shard_map/all_to_all | solution.py:617

commit v7 on v6

--- a/solution.py
+++ b/solution.py
@@ -198,7 +198,7 @@
     per_span = SPAN // CHUNK
     keeps = [None if k % per_span else keep_ref[k // per_span : k // per_span + 1, :] for k in range(chunks)]
     for k in range(chunks):
-        pad = padded.at[k % 4]
+        pad = padded.at[k % 8]
         fill_padded(pad, b_ref, none, k, slice(0, STATE), keeps[k])
         v = conv_ordered(pad, taps)
         if k == 0:
@@ -218,7 +218,7 @@
             toks = slice(k * CHUNK, (k + 1) * CHUNK)
             for part in range(LANES // 128):
                 cols = slice(part * 128, (part + 1) * 128)
-                pad = padded.at[(2 * k + part) % 4]
+                pad = padded.at[(2 * k + part) % 8]
                 fill_padded(pad, x_ref, none, k, cols, keeps[k])
                 v = conv_ordered(pad, weights[:, cols])
                 xs[i, toks, cols] = (v * wide[i, toks, cols]).astype(BF16)
@@ -280,7 +280,7 @@
         toks = slice(k * CHUNK, (k + 1) * CHUNK)
         pair = []
         for i, ref in enumerate((b_ref, c_ref)):
-            pad = padded.at[(2 * k + i) % 4]
+            pad = padded.at[(2 * k + i) % 8]
             fill_padded(pad, ref, edges[:, i * STATE : (i + 1) * STATE], k, slice(0, STATE), keeps[k])
             pair.append(conv_block(pad, wbc_ref[i].astype(F32) * 0.5))
         b, c = pair
@@ -339,7 +339,7 @@
         xs, direct = [], []
         for lane in range(0, LANES, 128):
             cols = slice(lane, lane + 128)
-            pad = padded.at[(2 * k + lane // 128) % 4]
+            pad = padded.at[(2 * k + lane // 128) % 8]
             fill_padded(pad, x_ref, edges[:, cols], k, cols, keeps[k])
             v = conv_block(pad, weights[:, cols])
             xs.append((v * wide_u[toks, cols]).astype(BF16))
@@ -378,8 +378,10 @@
     smalls = [(gain_hbm, gain_ref), (roll0_hbm, roll0_ref), (roll1_hbm, roll1_ref)]
     size = 2 * CHUNK
 
+    rows = out_all.shape[0] // 2
+
     def copy_in(i, m):
-        here = pl.ds(pl.multiple_of(m * size, size), size)
+        here = pl.ds(pl.multiple_of(m * rows, rows), rows)
         return pltpu.make_async_copy(pairs[i][0].at[here], pairs[i][1].at[here], in_sems.at[i, m])
 
     def copy_out(m):
@@ -389,7 +391,7 @@
     def copy_small(i):
         return pltpu.make_async_copy(*smalls[i], small_sems.at[i])
 
-    for m in range(chunks // 2):
+    for m in range(2):
         for i in range(len(pairs)):
             copy_in(i, m).start()
         if m == 0:
@@ -424,8 +426,6 @@
         copy_small(i).wait()
 
     def two(m, carry):
-        for i in range(len(pairs)):
-            copy_in(i, m).wait()
         scales = []
         for n in range(2):
 
@@ -450,7 +450,12 @@
         copy_out(m).start()
         return carry
 
-    lax.fori_loop(0, chunks // 2, two, 0)
+    def block(h, carry):
+        for i in range(len(pairs)):
+            copy_in(i, h).wait()
+        return lax.fori_loop(h * (chunks // 4), (h + 1) * (chunks // 4), two, carry)
+
+    lax.fori_loop(0, 2, block, 0)
     sums = [jnp.sum(parts[k].T, axis=0, keepdims=True) for k in range(chunks)]
     both = jnp.concatenate(sums + [roll0_ref[...] + roll1_ref[...]], axis=0)
     for i in range(sums_ref.shape[0]):
@@ -514,7 +519,7 @@
         name="tails",
     )(seq_spans, rank, x_values, b_values, c_values, b_values, steps_row, rate_row, conv_x, conv_bc)
     edge = lax.ppermute(edge, "seq", [(i, i + 1) for i in range(ring - 1)])
-    conv_scratch = pltpu.VMEM((4, 8 + CHUNK, 128), F32)
+    conv_scratch = pltpu.VMEM((8, 8 + CHUNK, 128), F32)
     wide_scratch = pltpu.VMEM((rows, LANES), F32)
 
     end, head_scale, chain, head = pl.pallas_call(
@@ -628,7 +633,7 @@
         + [pltpu.VMEM((1, width), F32)]
         + [pltpu.VMEM((chunks, CHUNK), F32)] * 2
         + [pltpu.VMEM((chunks, CHUNK, 128), F32)]
-        + [pltpu.SemaphoreType.DMA((3, chunks // 2))]
+        + [pltpu.SemaphoreType.DMA((3, 2))]
         + [pltpu.SemaphoreType.DMA((chunks // 2,)), pltpu.SemaphoreType.DMA((3,))],
         compiler_params=grant(24),
         cost_estimate=pl.CostEstimate(flops=1 << 28, bytes_accessed=8 << 20, transcendentals=1 << 10),

time: 67.8 us -> 67.5 us (level)
  transfers between devices with their start and end apart: 3 -> 3, of which waited for: 2 -> 2; matrix products, arithmetic and copies ran while one was open for 0% -> 0% of each run, Pallas kernels for 28% -> 27%
where the time goes in v7:
time: 67.5 us; the launch traced here: 67.2 us
  Pallas kernels  26.1 us (39%)
  starting transfers between devices  21.3 us (32%)
  blocking collectives  12.7 us (19%)
  waiting for transfers between devices  5.71 us (8%)
  between operations  0.7 us (1%)
    pallas_call x2, Pallas kernels, mix(): pl.pallas_call(functools.partial(mix_kernel, chunks, first * LANES), grid...  13.7 us
    all_to_all x1, blocking collectives, shards(): lax.all_to_all(sums, 'head', split_axis=0, concat_axis=0, tiled=True)  12.7 us
    all_to_all x1, starting transfers between devices, shards(): lax.all_to_all(msg, 'seq', split_axis=0, concat_axis=0, tiled=True)  10.1 us
    all_to_all x1, starting transfers between devices, shards(): lax.all_to_all(entering, 'seq', split_axis=0, concat_axis=0, tiled=True)  6.78 us
    pallas_call x1, Pallas kernels, shards(): pl.pallas_call(norm_kernel, in_specs=[vmem] * 4 + [hbm] * 6, out_specs=[h...  4.77 us
    pallas_call x1, Pallas kernels, shards(): pl.pallas_call(functools.partial(state_kernel, chunks), in_specs=[hbm] +...  4.76 us
    ppermute x1, starting transfers between devices, shards(): edge = lax.ppermute(edge, 'seq', [(i, i + 1) for i in range(ring - 1)])  4.37 us
    all_to_all x1, waiting for transfers between devices, shards(): lax.all_to_all(entering, 'seq', split_axis=0, concat_axis=0, tiled=True)  3.26 us
  transfers between devices with their start and end apart: 3, of which 2 were waited for; matrix products, arithmetic and copies ran while one was open for 0% of the time, Pallas kernels for 27%

profile of v7, /device:TPU:1, one launch (start us, length us, event | category | flops | bytes accessed | tf_op | source)
XLA Modules:
  0.0 67.2 jit_solution(2871216554108617786)
XLA Ops:
  0.6 1.1 %tails.1 = (bf16[16,1280]{1,0:T(8,128)(2,1)S(1)}, bf16[1024,128]{1,0:T(8,128)(2,1)S(1)}, f32[16,1024]{1,0:T(8,128)S(1)}, f32[1,16]{1,0:T(1,128)S(1)}, f32[8,1152]{1,0:T(8,128)S(1)}, /*index=5*/f32[8,128]{1,0:T(8,128)S(1)}) custom-call(s32[4]{0:T(128)} %seq_ref.5, s32[1]{0:T(128)} %bitcast.rank_ref, bf16[1024,1024]{1,0:T(8,128)(2,1)} %x_ref.5, ...), custom_call_target="tpu_custom_call" | custom-call | tf_op jit(solution)/shard_map/tails/pallas_call | solution.py:501
  1.7 4.4 %collective-permute-start = (bf16[16,1280]{1,0:T(8,128)(2,1)S(1)}, bf16[16,1280]{1,0:T(8,128)(2,1)S(1)}, u32[]{:S(2)}, u32[]{:S(2)}) collective-permute-start(bf16[16,1280]{1,0:T(8,128)(2,1)S(1)} %get-tuple-element.23), channel_id=1, source_target_pairs={{0,8},{8,16},{16,24},{24,32},{32,40},{40,48},{48,56},{56,64},{64,7... | collective-permute-start | bytes 122888 | tf_op jit(solution)/shard_map/ppermute | solution.py:521
  6.1 4.8 %states.1 = (f32[128,1024]{1,0:T(8,128)S(1)}, f32[16,1024]{1,0:T(8,128)S(1)}, f32[8,1024]{1,0:T(8,128)S(1)}, bf16[16,1152]{1,0:T(8,128)(2,1)S(1)}) custom-call(bf16[1024,1024]{1,0:T(8,128)(2,1)} %x_ref.5, bf16[1024,128]{1,0:T(8,128)(2,1)S(1)} %get-tuple-element.24.b_ref, f32[16,1024]{1,0:T(8,128)S(1)} %get-tuple-element.25.ts_ref, ...), custom_call_target="tpu_custom_call" | custom-call | flops 536870912 | bytes 4194304 | tf_op jit(solution)/shard_map/states/pallas_call | solution.py:525
  10.9 0.0 collective-permute-done.edge_ref.refs_2_
  10.9 1.1 %edge_states.1 = bf16[1088,128]{1,0:T(8,128)(2,1)} custom-call(bf16[16,1280]{1,0:T(8,128)(2,1)S(1)} %collective-permute-done.edge_ref.refs_2_, bf16[16,1152]{1,0:T(8,128)(2,1)S(1)} %get-tuple-element.29.head_ref, f32[8,1152]{1,0:T(8,128)S(1)} %get-tuple-element.27.taps_ref, f32[8,128]{1,0:T(8,128)S(1)} %get-tuple-element.28.keep_ref, ...), custom_call_target="tpu_custom_call" | custom-call | tf_op jit(solution)/shard_map/edge_states/pallas_call | solution.py:550
  11.9 10.1 %all-to-all-start = ((bf16[32,17,2,128]{3,2,1,0:T(2,128)(2,1)}), bf16[32,17,2,128]{3,2,1,0:T(2,128)(2,1)S(1)}, u32[]{:S(2)}, u32[]{:S(2)}) async-start(bf16[32,17,2,128]{3,2,1,0:T(2,128)(2,1)} %bitcast.3), calls=%async_computation | async-start | bytes 557056 | tf_op jit(solution)/shard_map/all_to_all | solution.py:560
  22.1 7.3 %mix_first.1 = (bf16[1024,512]{1,0:T(8,128)(2,1)}, bf16[1024,512]{1,0:T(8,128)(2,1)}, f32[8,128]{1,0:T(8,128)}, bf16[1024,256]{1,0:T(8,128)(2,1)}, bf16[8,128,12...) custom-call(s32[4]{0:T(128)} %seq_ref.5, s32[1]{0:T(128)} %bitcast.rank_ref, bf16[1024,1024]{1,0:T(8,128)(2,1)} %x_ref.5, ...), custom_call_target="tpu_custom_call" | custom-call | flops 1073741824 | bytes 9437184 | tf_op jit(solution)/shard_map/mix_first/pallas_call | solution.py:565
  29.3 2.5 %all-to-all-done = bf16[32,17,2,128]{3,2,1,0:T(2,128)(2,1)S(1)} async-done(((bf16[32,17,2,128]{3,2,1,0:T(2,128)(2,1)}), bf16[32,17,2,128]{3,2,1,0:T(2,128)(2,1)S(1)}, u32[]{:S(2)}, u32[]{:S(2)}) %all-to-all-start) | async-done | bytes 278560 | tf_op jit(solution)/shard_map/all_to_all | solution.py:560
  31.8 0.8 %scan.1 = bf16[32,32,128]{2,1,0:T(8,128)(2,1)} custom-call(bf16[1088,128]{1,0:T(8,128)(2,1)S(1)} %bitcast.9, f32[8,128]{1,0:T(8,128)} %get-tuple-element.33.after_ref.roll0_hbm), custom_call_target="tpu_custom_call" | custom-call | tf_op jit(solution)/shard_map/scan/pallas_call | solution.py:614
  32.6 6.8 %all-to-all-start.1 = ((bf16[32,32,128]{2,1,0:T(8,128)(2,1)}), bf16[32,32,128]{2,1,0:T(8,128)(2,1)S(1)}, u32[]{:S(2)}, u32[]{:S(2)}) async-start(bf16[32,32,128]{2,1,0:T(8,128)(2,1)} %scan.1), calls=%async_computation.1 | async-start | bytes 524288 | tf_op jit(solution)/shard_map/all_to_all | solution.py:622
  39.4 6.4 %mix_second.1 = (bf16[1024,512]{1,0:T(8,128)(2,1)S(1)}, bf16[1024,512]{1,0:T(8,128)(2,1)S(1)}, f32[8,128]{1,0:T(8,128)}) custom-call(s32[4]{0:T(128)} %seq_ref.5, s32[1]{0:T(128)} %bitcast.rank_ref, bf16[1024,1024]{1,0:T(8,128)(2,1)} %x_ref.5, bf16[16,1280]{1,0:T(8,128)(2,1)S(1)} %collective-permute-done.edge_ref.refs_2_, f32[16,1024]{1,0:T(8,128)} %bitcast.12, ...), custom_call_target="tpu_custom_call" | custom-call | flops 1073741824 | bytes 9437184 | tf_op jit(solution)/shard_map/mix_second/pallas_call | solution.py:565
  45.8 3.3 %all-to-all-done.1.in_ref = bf16[32,32,128]{2,1,0:T(8,128)(2,1)S(1)} async-done(((bf16[32,32,128]{2,1,0:T(8,128)(2,1)}), bf16[32,32,128]{2,1,0:T(8,128)(2,1)S(1)}, u32[]{:S(2)}, u32[]{:S(2)}) %all-to-all-start.1) | async-done | bytes 262176 | tf_op jit(solution)/shard_map/all_to_all | solution.py:622
  49.0 4.8 %norms.1 = (bf16[1024,1024]{1,0:T(8,128)(2,1)}, f32[8,16,128]{2,1,0:T(8,128)S(1)}) custom-call(bf16[32,32,128]{2,1,0:T(8,128)(2,1)S(1)} %all-to-all-done.1.in_ref, bf16[1024,512]{1,0:T(8,128)(2,1)S(1)} %get-tuple-element.36.a1_all, bf16[1024,512]{1,0:T(8,128)(2,1)S(1)} %get-tuple-element.37.f1_all, bf16[1024,128]{1,0:T(8,128)(2,1)S(1)} %get-tuple-element.38.cc_ref, ...), custom_call_target="tpu_custom_call" | custom-call | flops 268435456 | bytes 8388608 | tf_op jit(solution)/shard_map/norms/pallas_call | solution.py:625
  53.8 12.7 %all_to_all.15 = f32[8,16,128]{2,1,0:T(8,128)S(1)} all-to-all(f32[8,16,128]{2,1,0:T(8,128)S(1)} %get-tuple-element.43), channel_id=1, replica_groups=mesh['seq'=32,'head'=8] {'head'}, dimensions={0} | all-to-all | bytes 131072 | tf_op jit(solution)/shard_map/all_to_all | solution.py:643
  66.6 0.6 fusion.2
  (1 shorter events, 0.0 us)
Async XLA Ops:
  1.7 9.1 %collective-permute-start = (bf16[16,1280]{1,0:T(8,128)(2,1)S(1)}, bf16[16,1280]{1,0:T(8,128)(2,1)S(1)}, u32[]{:S(2)}, u32[]{:S(2)}) collective-permute-start(bf16[16,1280]{1,0:T(8,128)(2,1)S(1)} %get-tuple-element.23), channel_id=1, source_target_pairs={{0,8},{8,16},{16,24},{24,32},{32,40},{40,48},{48,56},{56,64},{64,7... | collective-permute-start | bytes 122888 | tf_op jit(solution)/shard_map/ppermute | solution.py:521
  11.9 19.9 %all-to-all-start = ((bf16[32,17,2,128]{3,2,1,0:T(2,128)(2,1)}), bf16[32,17,2,128]{3,2,1,0:T(2,128)(2,1)S(1)}, u32[]{:S(2)}, u32[]{:S(2)}) async-start(bf16[32,17,2,128]{3,2,1,0:T(2,128)(2,1)} %bitcast.3), calls=%async_computation | async-start | bytes 557056 | tf_op jit(solution)/shard_map/all_to_all | solution.py:560
  32.6 16.5 %all-to-all-start.1 = ((bf16[32,32,128]{2,1,0:T(8,128)(2,1)}), bf16[32,32,128]{2,1,0:T(8,128)(2,1)S(1)}, u32[]{:S(2)}, u32[]{:S(2)}) async-start(bf16[32,32,128]{2,1,0:T(8,128)(2,1)} %scan.1), calls=%async_computation.1 | async-start | bytes 524288 | tf_op jit(solution)/shard_map/all_to_all | solution.py:622

commit v8 on v7

--- a/solution.py
+++ b/solution.py
@@ -411,8 +411,8 @@
         return squares
 
     def near(m, carry):
-        for n in range(2):
-            k = 2 * m + n
+        for n in range(4):
+            k = 4 * m + n
             toks = pl.ds(pl.multiple_of(k * CHUNK, CHUNK), CHUNK)
 
             def put(cols, g):
@@ -421,7 +421,7 @@
             parts[k] = gate(k, range(half, width, LANES), a1_all, f1_all, put, jnp.zeros((CHUNK, 128), F32))
         return carry
 
-    lax.fori_loop(0, chunks // 2, near, 0)
+    lax.fori_loop(0, chunks // 4, near, 0)
     for i in range(len(smalls)):
         copy_small(i).wait()
 

time: 67.5 us -> 67.5 us (level)
  no operation moved by 1% of the time
where the time goes in v8:
time: 67.5 us; the launch traced here: 67.2 us
  Pallas kernels  26.1 us (39%)
  starting transfers between devices  21.3 us (32%)
  blocking collectives  12.7 us (19%)
  waiting for transfers between devices  5.71 us (8%)
  between operations  0.7 us (1%)
    pallas_call x2, Pallas kernels, mix(): pl.pallas_call(functools.partial(mix_kernel, chunks, first * LANES), grid...  13.7 us
    all_to_all x1, blocking collectives, shards(): lax.all_to_all(sums, 'head', split_axis=0, concat_axis=0, tiled=True)  12.7 us
    all_to_all x1, starting transfers between devices, shards(): lax.all_to_all(msg, 'seq', split_axis=0, concat_axis=0, tiled=True)  10.1 us
    all_to_all x1, starting transfers between devices, shards(): lax.all_to_all(entering, 'seq', split_axis=0, concat_axis=0, tiled=True)  6.78 us
    pallas_call x1, Pallas kernels, shards(): pl.pallas_call(norm_kernel, in_specs=[vmem] * 4 + [hbm] * 6, out_specs=[h...  4.77 us
    pallas_call x1, Pallas kernels, shards(): pl.pallas_call(functools.partial(state_kernel, chunks), in_specs=[hbm] +...  4.76 us
    ppermute x1, starting transfers between devices, shards(): edge = lax.ppermute(edge, 'seq', [(i, i + 1) for i in range(ring - 1)])  4.37 us
    all_to_all x1, waiting for transfers between devices, shards(): lax.all_to_all(entering, 'seq', split_axis=0, concat_axis=0, tiled=True)  3.26 us
  transfers between devices with their start and end apart: 3, of which 2 were waited for; matrix products, arithmetic and copies ran while one was open for 0% of the time, Pallas kernels for 27%

profile of v8, /device:TPU:1, one launch (start us, length us, event | category | flops | bytes accessed | tf_op | source)
XLA Modules:
  0.0 67.2 jit_solution(17695695755268611416)
XLA Ops:
  0.6 1.1 %tails.1 = (bf16[16,1280]{1,0:T(8,128)(2,1)S(1)}, bf16[1024,128]{1,0:T(8,128)(2,1)S(1)}, f32[16,1024]{1,0:T(8,128)S(1)}, f32[1,16]{1,0:T(1,128)S(1)}, f32[8,1152]{1,0:T(8,128)S(1)}, /*index=5*/f32[8,128]{1,0:T(8,128)S(1)}) custom-call(s32[4]{0:T(128)} %seq_ref.5, s32[1]{0:T(128)} %bitcast.rank_ref, bf16[1024,1024]{1,0:T(8,128)(2,1)} %x_ref.5, ...), custom_call_target="tpu_custom_call" | custom-call | tf_op jit(solution)/shard_map/tails/pallas_call | solution.py:501
  1.7 4.4 %collective-permute-start = (bf16[16,1280]{1,0:T(8,128)(2,1)S(1)}, bf16[16,1280]{1,0:T(8,128)(2,1)S(1)}, u32[]{:S(2)}, u32[]{:S(2)}) collective-permute-start(bf16[16,1280]{1,0:T(8,128)(2,1)S(1)} %get-tuple-element.23), channel_id=1, source_target_pairs={{0,8},{8,16},{16,24},{24,32},{32,40},{40,48},{48,56},{56,64},{64,7... | collective-permute-start | bytes 122888 | tf_op jit(solution)/shard_map/ppermute | solution.py:521
  6.1 4.8 %states.1 = (f32[128,1024]{1,0:T(8,128)S(1)}, f32[16,1024]{1,0:T(8,128)S(1)}, f32[8,1024]{1,0:T(8,128)S(1)}, bf16[16,1152]{1,0:T(8,128)(2,1)S(1)}) custom-call(bf16[1024,1024]{1,0:T(8,128)(2,1)} %x_ref.5, bf16[1024,128]{1,0:T(8,128)(2,1)S(1)} %get-tuple-element.24.b_ref, f32[16,1024]{1,0:T(8,128)S(1)} %get-tuple-element.25.ts_ref, ...), custom_call_target="tpu_custom_call" | custom-call | flops 536870912 | bytes 4194304 | tf_op jit(solution)/shard_map/states/pallas_call | solution.py:525
  10.9 0.0 collective-permute-done.edge_ref.refs_2_
  10.9 1.1 %edge_states.1 = bf16[1088,128]{1,0:T(8,128)(2,1)} custom-call(bf16[16,1280]{1,0:T(8,128)(2,1)S(1)} %collective-permute-done.edge_ref.refs_2_, bf16[16,1152]{1,0:T(8,128)(2,1)S(1)} %get-tuple-element.29.head_ref, f32[8,1152]{1,0:T(8,128)S(1)} %get-tuple-element.27.taps_ref, f32[8,128]{1,0:T(8,128)S(1)} %get-tuple-element.28.keep_ref, ...), custom_call_target="tpu_custom_call" | custom-call | tf_op jit(solution)/shard_map/edge_states/pallas_call | solution.py:550
  11.9 10.1 %all-to-all-start = ((bf16[32,17,2,128]{3,2,1,0:T(2,128)(2,1)}), bf16[32,17,2,128]{3,2,1,0:T(2,128)(2,1)S(1)}, u32[]{:S(2)}, u32[]{:S(2)}) async-start(bf16[32,17,2,128]{3,2,1,0:T(2,128)(2,1)} %bitcast.3), calls=%async_computation | async-start | bytes 557056 | tf_op jit(solution)/shard_map/all_to_all | solution.py:560
  22.1 7.3 %mix_first.1 = (bf16[1024,512]{1,0:T(8,128)(2,1)}, bf16[1024,512]{1,0:T(8,128)(2,1)}, f32[8,128]{1,0:T(8,128)}, bf16[1024,256]{1,0:T(8,128)(2,1)}, bf16[8,128,12...) custom-call(s32[4]{0:T(128)} %seq_ref.5, s32[1]{0:T(128)} %bitcast.rank_ref, bf16[1024,1024]{1,0:T(8,128)(2,1)} %x_ref.5, ...), custom_call_target="tpu_custom_call" | custom-call | flops 1073741824 | bytes 9437184 | tf_op jit(solution)/shard_map/mix_first/pallas_call | solution.py:565
  29.3 2.5 %all-to-all-done = bf16[32,17,2,128]{3,2,1,0:T(2,128)(2,1)S(1)} async-done(((bf16[32,17,2,128]{3,2,1,0:T(2,128)(2,1)}), bf16[32,17,2,128]{3,2,1,0:T(2,128)(2,1)S(1)}, u32[]{:S(2)}, u32[]{:S(2)}) %all-to-all-start) | async-done | bytes 278560 | tf_op jit(solution)/shard_map/all_to_all | solution.py:560
  31.8 0.8 %scan.1 = bf16[32,32,128]{2,1,0:T(8,128)(2,1)} custom-call(bf16[1088,128]{1,0:T(8,128)(2,1)S(1)} %bitcast.9, f32[8,128]{1,0:T(8,128)} %get-tuple-element.33.after_ref.roll0_hbm), custom_call_target="tpu_custom_call" | custom-call | tf_op jit(solution)/shard_map/scan/pallas_call | solution.py:614
  32.6 6.8 %all-to-all-start.1 = ((bf16[32,32,128]{2,1,0:T(8,128)(2,1)}), bf16[32,32,128]{2,1,0:T(8,128)(2,1)S(1)}, u32[]{:S(2)}, u32[]{:S(2)}) async-start(bf16[32,32,128]{2,1,0:T(8,128)(2,1)} %scan.1), calls=%async_computation.1 | async-start | bytes 524288 | tf_op jit(solution)/shard_map/all_to_all | solution.py:622
  39.4 6.4 %mix_second.1 = (bf16[1024,512]{1,0:T(8,128)(2,1)S(1)}, bf16[1024,512]{1,0:T(8,128)(2,1)S(1)}, f32[8,128]{1,0:T(8,128)}) custom-call(s32[4]{0:T(128)} %seq_ref.5, s32[1]{0:T(128)} %bitcast.rank_ref, bf16[1024,1024]{1,0:T(8,128)(2,1)} %x_ref.5, bf16[16,1280]{1,0:T(8,128)(2,1)S(1)} %collective-permute-done.edge_ref.refs_2_, f32[16,1024]{1,0:T(8,128)} %bitcast.12, ...), custom_call_target="tpu_custom_call" | custom-call | flops 1073741824 | bytes 9437184 | tf_op jit(solution)/shard_map/mix_second/pallas_call | solution.py:565
  45.8 3.3 %all-to-all-done.1.in_ref = bf16[32,32,128]{2,1,0:T(8,128)(2,1)S(1)} async-done(((bf16[32,32,128]{2,1,0:T(8,128)(2,1)}), bf16[32,32,128]{2,1,0:T(8,128)(2,1)S(1)}, u32[]{:S(2)}, u32[]{:S(2)}) %all-to-all-start.1) | async-done | bytes 262176 | tf_op jit(solution)/shard_map/all_to_all | solution.py:622
  49.0 4.8 %norms.1 = (bf16[1024,1024]{1,0:T(8,128)(2,1)}, f32[8,16,128]{2,1,0:T(8,128)S(1)}) custom-call(bf16[32,32,128]{2,1,0:T(8,128)(2,1)S(1)} %all-to-all-done.1.in_ref, bf16[1024,512]{1,0:T(8,128)(2,1)S(1)} %get-tuple-element.36.a1_all, bf16[1024,512]{1,0:T(8,128)(2,1)S(1)} %get-tuple-element.37.f1_all, bf16[1024,128]{1,0:T(8,128)(2,1)S(1)} %get-tuple-element.38.cc_ref, ...), custom_call_target="tpu_custom_call" | custom-call | flops 268435456 | bytes 8388608 | tf_op jit(solution)/shard_map/norms/pallas_call | solution.py:625
  53.8 12.7 %all_to_all.15 = f32[8,16,128]{2,1,0:T(8,128)S(1)} all-to-all(f32[8,16,128]{2,1,0:T(8,128)S(1)} %get-tuple-element.43), channel_id=1, replica_groups=mesh['seq'=32,'head'=8] {'head'}, dimensions={0} | all-to-all | bytes 131072 | tf_op jit(solution)/shard_map/all_to_all | solution.py:643
  66.6 0.6 fusion.2
  (1 shorter events, 0.0 us)
Async XLA Ops:
  1.7 9.1 %collective-permute-start = (bf16[16,1280]{1,0:T(8,128)(2,1)S(1)}, bf16[16,1280]{1,0:T(8,128)(2,1)S(1)}, u32[]{:S(2)}, u32[]{:S(2)}) collective-permute-start(bf16[16,1280]{1,0:T(8,128)(2,1)S(1)} %get-tuple-element.23), channel_id=1, source_target_pairs={{0,8},{8,16},{16,24},{24,32},{32,40},{40,48},{48,56},{56,64},{64,7... | collective-permute-start | bytes 122888 | tf_op jit(solution)/shard_map/ppermute | solution.py:521
  11.9 19.9 %all-to-all-start = ((bf16[32,17,2,128]{3,2,1,0:T(2,128)(2,1)}), bf16[32,17,2,128]{3,2,1,0:T(2,128)(2,1)S(1)}, u32[]{:S(2)}, u32[]{:S(2)}) async-start(bf16[32,17,2,128]{3,2,1,0:T(2,128)(2,1)} %bitcast.3), calls=%async_computation | async-start | bytes 557056 | tf_op jit(solution)/shard_map/all_to_all | solution.py:560
  32.6 16.5 %all-to-all-start.1 = ((bf16[32,32,128]{2,1,0:T(8,128)(2,1)}), bf16[32,32,128]{2,1,0:T(8,128)(2,1)S(1)}, u32[]{:S(2)}, u32[]{:S(2)}) async-start(bf16[32,32,128]{2,1,0:T(8,128)(2,1)} %scan.1), calls=%async_computation.1 | async-start | bytes 524288 | tf_op jit(solution)/shard_map/all_to_all | solution.py:622
